TPU v7x, 128 devices: a whole 4x4x4 slice. The times are simulated.
128 devices in a mesh: row: 4 (over z), col: 32 (over x, y, core).
Axes of the slice: x: 4, y: 4, z: 4, core: 2. Of those that a mesh axis runs over, the one named last changes fastest.
Arguments:
- object_field: float32 [2, 4, 1024, 8192], P(None, None, 'row', 'col'), may hold values from -4 to 4
- probe: float32 [2, 4, 128, 128], replicated, may hold values from -6 to 6
- amplitudes: float32 [4, 32, 5, 128, 128], P('row', 'col'), may hold values from 0.2 to 4
- offsets: int32 [4, 32, 5, 2], P('row', 'col'), may hold values from 0 to 8064, as said below
- counts: int32 [4, 32], P('row', 'col'), may hold values from 1 to 5, as said below
Outputs:
- new_object: float32 [2, 4, 1024, 8192], P(None, None, 'row', 'col')
- new_probe: float32 [2, 4, 128, 128], replicated
Inputs may be any that keep to these rules, and one draw needn't show every extreme that they name: `offsets`: slot k of device (a, b) has corner (y, x) with a * 256 <= y < (a + 1) * 256, b * 256 <= x < (b + 1) * 256, y <= 896 and x <= 8064; dead slots hold such corners too. Slots k >= counts of a device are dead; some device has all 5 slots live.
All inputs are finite; a program needn't handle non-finite values.
Results may differ from a plain program's by a relative error of at most 0.00019.
Values sent between devices are 32-bit elements; how exact they have to be, the bound alone decides.
No kernel may reach another device: no remote copies, remote signals or barrier semaphores. Data moves between devices by JAX's collectives and lax.ppermute only.
A program may use at most 128 MiB of HBM per device.

v0:
```python
from functools import partial
import math

import jax
import jax.numpy as jnp
from jax import lax
from jax.sharding import PartitionSpec as P

FRESNEL = 4.0
STEP_OBJECT = 0.5
STEP_PROBE = 0.5


def shifted(value, axis, steps):
    count = lax.axis_size(axis)
    leading, last = (max(0, -steps), min(count, count - steps))
    return lax.ppermute(value, axis, [(source, source + steps) for source in range(leading, last)])


def dft_tables(points):
    position = jnp.arange(points, dtype=jnp.int32)
    product = position[:, None] * position[None, :] % points
    angle = -2.0 * math.pi / points * product.astype(jnp.float32)
    norm_factor = 1.0 / math.sqrt(points)
    frequency = (
        jnp.where(position < points // 2, position, position - points).astype(jnp.float32) / points
    )
    phase = -math.pi * FRESNEL * (frequency[:, None] ** 2 + frequency[None, :] ** 2)
    return (
        jnp.cos(angle) * norm_factor,
        jnp.sin(angle) * norm_factor,
        jnp.cos(phase),
        jnp.sin(phase),
    )


def product_left(table_real, table_imag, field_real, field_imag):
    contract = partial(jnp.einsum, precision=lax.Precision.HIGHEST)
    real_part = contract("jk,mkl->mjl", table_real, field_real) - contract(
        "jk,mkl->mjl", table_imag, field_imag
    )
    imag_part = contract("jk,mkl->mjl", table_real, field_imag) + contract(
        "jk,mkl->mjl", table_imag, field_real
    )
    return (real_part, imag_part)


def product_right(field_real, field_imag, table_real, table_imag):
    contract = partial(jnp.einsum, precision=lax.Precision.HIGHEST)
    real_part = contract("mjk,kl->mjl", field_real, table_real) - contract(
        "mjk,kl->mjl", field_imag, table_imag
    )
    imag_part = contract("mjk,kl->mjl", field_real, table_imag) + contract(
        "mjk,kl->mjl", field_imag, table_real
    )
    return (real_part, imag_part)


def transform(field_real, field_imag, table_real, table_imag):
    mixed_real, mixed_imag = product_left(table_real, table_imag, field_real, field_imag)
    return product_right(mixed_real, mixed_imag, table_real, table_imag)


def position_loss(window, probe, amplitude, tables):
    table_real, table_imag, kernel_real, kernel_imag = tables
    wave_real = probe[0]
    wave_imag = probe[1]
    depth = window.shape[1]
    for slice_index in range(depth):
        object_real = window[0, slice_index]
        object_imag = window[1, slice_index]
        wave_real, wave_imag = (
            wave_real * object_real - wave_imag * object_imag,
            wave_real * object_imag + wave_imag * object_real,
        )
        if slice_index < depth - 1:
            spec_real, spec_imag = transform(wave_real, wave_imag, table_real, table_imag)
            spec_real, spec_imag = (
                spec_real * kernel_real - spec_imag * kernel_imag,
                spec_real * kernel_imag + spec_imag * kernel_real,
            )
            wave_real, wave_imag = transform(spec_real, spec_imag, table_real, -table_imag)
    far_real, far_imag = transform(wave_real, wave_imag, table_real, table_imag)
    intensity = jnp.sum(far_real**2 + far_imag**2, axis=0)
    return jnp.sum((jnp.sqrt(intensity + 1.0) - amplitude) ** 2)


def shards(object_field, probe, amplitudes, offsets, counts):
    tile_rows = object_field.shape[2]
    tile_cols = object_field.shape[3]
    depth = object_field.shape[1]
    points = probe.shape[2]
    slot_count = offsets.shape[2]
    row_index = lax.axis_index("row")
    col_index = lax.axis_index("col")
    below = shifted(object_field[:, :, :points, :], "row", -1)
    rows_extended = jnp.concatenate([object_field, below], axis=2)
    right_rim = shifted(rows_extended[:, :, :, :points], "col", -1)
    extended = jnp.concatenate([rows_extended, right_rim], axis=3)
    tables = dft_tables(points)
    local_rows = offsets[0, 0, :, 0] - row_index * tile_rows
    local_cols = offsets[0, 0, :, 1] - col_index * tile_cols

    def cut_window(start_row, start_col):
        return lax.dynamic_slice(extended, (0, 0, start_row, start_col), (2, depth, points, points))

    windows = jax.vmap(cut_window)(local_rows, local_cols)
    alive = (jnp.arange(slot_count, dtype=jnp.int32) < counts[0, 0]).astype(jnp.float32)
    target = amplitudes[0, 0]

    def total_loss(window_batch, probe_part):
        losses = jax.vmap(position_loss, in_axes=(0, None, 0, None))(
            window_batch, probe_part, target, tables
        )
        return jnp.sum(alive * losses)

    loss_value, pull_back = jax.vjp(total_loss, windows, probe)
    grad_windows, grad_probe = pull_back(jnp.ones((), jnp.float32))
    weight = jnp.sum(alive[:, None, None] * (windows[:, 0, 0] ** 2 + windows[:, 1, 0] ** 2), axis=0)
    grad_ext = jnp.zeros((2, depth, tile_rows + points, tile_cols + points), jnp.float32)
    for slot_index in range(slot_count):
        starts = (0, 0, local_rows[slot_index], local_cols[slot_index])
        previous = lax.dynamic_slice(grad_ext, starts, (2, depth, points, points))
        grad_ext = lax.dynamic_update_slice(grad_ext, previous + grad_windows[slot_index], starts)
    returned = shifted(grad_ext[:, :, :, tile_cols:], "col", 1)
    grad_ext = grad_ext.at[:, :, :, :points].add(returned)
    lower_back = shifted(grad_ext[:, :, tile_rows:, :tile_cols], "row", 1)
    grad_tile = grad_ext[:, :, :tile_rows, :tile_cols].at[:, :, :points, :].add(lower_back)
    new_object = object_field - STEP_OBJECT * grad_tile
    grad_total, weight_total = lax.psum((grad_probe, weight), ("row", "col"))
    new_probe = probe - STEP_PROBE * grad_total / (weight_total + 1.0)
    return (new_object, new_probe)


def solution(mesh):
    return jax.shard_map(
        shards,
        mesh=mesh,
        in_specs=(
            P(None, None, "row", "col"),
            P(),
            P("row", "col", None, None, None),
            P("row", "col", None, None),
            P("row", "col"),
        ),
        out_specs=(P(None, None, "row", "col"), P()),
        check_vma=False,
    )
```

profile of v0, /device:TPU:1, one launch (start us, length us, event | category | flops | bytes accessed | tf_op | source)
XLA Modules:
  0.0 577.1 jit_solution(16020343173458893665)
XLA Ops:
  10.1 25.8 %collective-permute-done = f32[2,4,128,256]{3,2,1,0:T(8,128)S(1)} collective-permute-done((f32[2,4,128,256]{3,2,1,0:T(8,128)S(1)}, f32[2,4,128,256]{3,2,1,0:T(8,128)S(1)}, u32[]{:S(2)}, u32[]{:S(2)}) %collective-permute-start) | collective-permute-done | bytes 1048608 | tf_op jit(solution)/shard_map/ppermute | solution.py:17
  37.2 3.1 collective-permute-start.1
  65.7 3.9 pad_maximum_fusion
  69.5 21.1 %while.3 = (s32[]{:T(128)}, f32[2,4,384,384]{3,2,1,0:T(8,128)}, s32[5,4]{0,1:T(4,128)S(1)}, f32[5,2,4,128,128]{4,3,2,1,0:T(8,128)}, s32[]{:T(128)}) while((s32[]{:T(128)}, f32[2,4,384,384]{3,2,1,0:T(8,128)}, s32[5,4]{0,1:T(4,128)S(1)}, f32[5,2,4,128,128]{4,3,2,1,0:T(8,128)}, s32[]{:T(128)}) %tuple.86), condition=%wide.while_cond.2, body=%wide.while_body.2.sunk | while | flops 2 | bytes 1049725 | solution.py:105
  70.1 3.6 bitcast_dynamic-update-slice_fusion.2
  74.3 3.6 bitcast_dynamic-update-slice_fusion.2
  78.5 3.6 bitcast_dynamic-update-slice_fusion.2
  82.7 3.6 bitcast_dynamic-update-slice_fusion.2
  86.9 3.6 bitcast_dynamic-update-slice_fusion.2
  156.0 2.9 fusion.7
  193.4 2.9 fusion.94
  242.1 3.2 multiply_reduce_fusion.18
  269.2 3.0 multiply_reduce_fusion.14
  295.8 3.1 multiply_reduce_fusion.10
  325.2 4.2 multiply_reduce_fusion.3
  337.6 7.3 %dynamic_update_slice.15 = f32[2,4,384,384]{3,2,1,0:T(8,128)} dynamic-update-slice(f32[2,4,384,384]{3,2,1,0:T(8,128)} %broadcast_in_dim.2, f32[2,4,128,128]{3,2,1,0:T(8,128)S(1)} %slice_bitcast_fusion.4, s32[]{:T(128)} %constant.94.clone.1, s32[]{:T(128)} %constant.94.clone.1, s32[]{:T(128)S(6)} %select_n.349, s32[]{:T(128)S(6)} %select_n.350) | dynamic-update-slice | bytes 1048580 | tf_op jit(solution)/shard_map/dynamic_update_slice | solution.py:124
  346.3 7.4 %dynamic_update_slice.16 = f32[2,4,384,384]{3,2,1,0:T(8,128)} dynamic-update-slice(f32[2,4,384,384]{3,2,1,0:T(8,128)} %dynamic_update_slice.15, f32[2,4,128,128]{3,2,1,0:T(8,128)S(1)} %fusion.89, s32[]{:T(128)} %constant.94.clone.1, s32[]{:T(128)} %constant.94.clone.1, s32[]{:T(128)S(6)} %select_n.351, s32[]{:T(128)S(6)} %select_n.352) | dynamic-update-slice | bytes 1048580 | tf_op jit(solution)/shard_map/dynamic_update_slice | solution.py:124
  355.2 7.7 %dynamic_update_slice.17 = f32[2,4,384,384]{3,2,1,0:T(8,128)} dynamic-update-slice(f32[2,4,384,384]{3,2,1,0:T(8,128)} %dynamic_update_slice.16, f32[2,4,128,128]{3,2,1,0:T(8,128)S(1)} %fusion.88, s32[]{:T(128)} %constant.94.clone.1, s32[]{:T(128)} %constant.94.clone.1, s32[]{:T(128)S(6)} %select_n.353, s32[]{:T(128)S(6)} %select_n.354) | dynamic-update-slice | bytes 1048580 | tf_op jit(solution)/shard_map/dynamic_update_slice | solution.py:124
  364.4 8.0 %dynamic_update_slice.18 = f32[2,4,384,384]{3,2,1,0:T(8,128)} dynamic-update-slice(f32[2,4,384,384]{3,2,1,0:T(8,128)} %dynamic_update_slice.17, f32[2,4,128,128]{3,2,1,0:T(8,128)S(1)} %fusion.87, s32[]{:T(128)} %constant.94.clone.1, s32[]{:T(128)} %constant.94.clone.1, s32[]{:T(128)S(6)} %select_n.355, s32[]{:T(128)S(6)} %select_n.356) | dynamic-update-slice | bytes 1048580 | tf_op jit(solution)/shard_map/dynamic_update_slice | solution.py:124
  373.9 7.8 %dynamic_update_slice.19 = f32[2,4,384,384]{3,2,1,0:T(8,128)} dynamic-update-slice(f32[2,4,384,384]{3,2,1,0:T(8,128)} %dynamic_update_slice.18, f32[2,4,128,128]{3,2,1,0:T(8,128)S(1)} %fusion.86, s32[]{:T(128)} %constant.94.clone.1, s32[]{:T(128)} %constant.94.clone.1, s32[]{:T(128)S(6)} %select_n.357, s32[]{:T(128)S(6)} %select_n.358) | dynamic-update-slice | bytes 1048580 | tf_op jit(solution)/shard_map/dynamic_update_slice | solution.py:124
  383.4 3.5 collective-permute-start.2
  387.0 17.2 %collective-permute-done.2 = f32[2,4,384,128]{3,2,1,0:T(8,128)S(1)} collective-permute-done((f32[2,4,384,128]{3,2,1,0:T(8,128)S(1)}, f32[2,4,384,128]{3,2,1,0:T(8,128)S(1)}, u32[]{:S(2)}, u32[]{:S(2)}) %collective-permute-start.2) | collective-permute-done | bytes 1572896 | tf_op jit(solution)/shard_map/ppermute | solution.py:17
  406.8 2.8 collective-permute-start.3
  412.5 149.0 %all-reduce.13.cloned.1.call-done = (f32[2,4,128,128]{2,3,1,0:T(8,128)}, f32[128,128]{1,0:T(8,128)}) async-done(((f32[2,4,128,128]{2,3,1,0:T(8,128)}, f32[128,128]{1,0:T(8,128)}), (f32[2,4,128,128]{2,3,1,0:T(8,128)}, f32[128,128]{1,0:T(8,128)})) %all-reduce.13.cloned.1.call-update) | async-done | bytes 589840 | tf_op jit(solution)/shard_map/psum | solution.py:130
  (226 shorter events, 261.2 us)
Async XLA Ops:
  7.2 554.3 %all-reduce.13.cloned.1.call-start = ((), (), s32[]{:S(2)}) async-start(), calls=%async_computation | async-start | bytes 1179648 | tf_op jit(solution)/shard_map/psum | solution.py:130
  7.2 2.8 copy-start.2
  8.7 27.2 %collective-permute-start = (f32[2,4,128,256]{3,2,1,0:T(8,128)S(1)}, f32[2,4,128,256]{3,2,1,0:T(8,128)S(1)}, u32[]{:S(2)}, u32[]{:S(2)}) collective-permute-start(f32[2,4,128,256]{3,2,1,0:T(8,128)S(1)} %slice.168), channel_id=1, source_target_pairs={{32,0},{64,32},{96,64},{33,1},{65,33},{97,65},{34,2},{66,34},{98,6... | collective-permute-start | bytes 3145736 | tf_op jit(solution)/shard_map/ppermute | solution.py:17
  36.0 4.4 copy-start.26
  37.2 28.4 %collective-permute-start.1 = (f32[2,4,384,128]{3,2,1,0:T(8,128)}, f32[2,4,384,128]{3,2,1,0:T(8,128)}, u32[]{:S(2)}, u32[]{:S(2)}) collective-permute-start(f32[2,4,384,128]{3,2,1,0:T(8,128)} %slice.220), channel_id=1, source_target_pairs={{1,0},{2,1},{3,2},{4,3},{5,4},{6,5},{7,6},{8,7},{9,8},{10,9},{11,1... | collective-permute-start | bytes 4718600 | tf_op jit(solution)/shard_map/ppermute | solution.py:17
  94.1 1.3 copy-start.4
  228.4 2.5 copy-start.25
  329.3 3.6 copy-start.6
  329.3 3.6 copy-start.7
  329.3 3.6 copy-start.8
  329.3 3.6 copy-start.9
  332.0 1.3 copy-start.12
  333.1 1.3 copy-start.16
  333.4 1.4 copy-start.20
  373.9 13.0 %copy-start.21 = (f32[4,128,128]{1,2,0:T(8,128)S(1)}, f32[4,128,128]{1,2,0:T(8,128)}, u32[]{:S(2)}) copy-start(f32[4,128,128]{1,2,0:T(8,128)} %get-tuple-element.42) | copy-start | bytes 786436
  373.9 13.0 %copy-start.22 = (f32[4,128,128]{1,2,0:T(8,128)S(1)}, f32[4,128,128]{1,2,0:T(8,128)}, u32[]{:S(2)}) copy-start(f32[4,128,128]{1,2,0:T(8,128)} %get-tuple-element.43) | copy-start | bytes 786436
  373.9 13.0 %copy-start.23 = (f32[4,128,128]{1,2,0:T(8,128)S(1)}, f32[4,128,128]{1,2,0:T(8,128)}, u32[]{:S(2)}) copy-start(f32[4,128,128]{1,2,0:T(8,128)} %get-tuple-element.60) | copy-start | bytes 786436
  373.9 13.0 %copy-start.24 = (f32[4,128,128]{1,2,0:T(8,128)S(1)}, f32[4,128,128]{1,2,0:T(8,128)}, u32[]{:S(2)}) copy-start(f32[4,128,128]{1,2,0:T(8,128)} %get-tuple-element.61) | copy-start | bytes 786436
  381.7 22.5 %copy-start = (f32[2,4,384,384]{3,2,1,0:T(8,128)S(1)}, f32[2,4,384,384]{3,2,1,0:T(8,128)}, u32[]{:S(2)}) copy-start(f32[2,4,384,384]{3,2,1,0:T(8,128)} %dynamic_update_slice.19) | copy-start | bytes 14155780
  383.4 20.8 %collective-permute-start.2 = (f32[2,4,384,128]{3,2,1,0:T(8,128)S(1)}, f32[2,4,384,128]{3,2,1,0:T(8,128)S(1)}, u32[]{:S(2)}, u32[]{:S(2)}) collective-permute-start(f32[2,4,384,128]{3,2,1,0:T(8,128)S(1)} %slice.228), channel_id=1, source_target_pairs={{0,1},{1,2},{2,3},{3,4},{4,5},{5,6},{6,7},{7,8},{8,9},{9,10},{10,1... | collective-permute-start | bytes 4718600 | tf_op jit(solution)/shard_map/ppermute | solution.py:17
  404.6 2.1 copy-start.1
  406.8 5.5 copy-start.5
  406.8 159.6 %collective-permute-start.3 = (f32[2,4,128,256]{3,2,1,0:T(8,128)S(1)}, f32[2,4,128,256]{3,2,1,0:T(8,128)S(1)}, u32[]{:S(2)}, u32[]{:S(2)}) collective-permute-start(f32[2,4,128,256]{3,2,1,0:T(8,128)S(1)} %slice.231), channel_id=1, source_target_pairs={{0,32},{32,64},{64,96},{1,33},{33,65},{65,97},{2,34},{34,66},{66,9... | collective-permute-start | bytes 3145736 | tf_op jit(solution)/shard_map/ppermute | solution.py:17
  566.4 1.9 copy-start.3
  (8 other events, 9.0 us)
Sparse Core Ops, SparseCore 0:
  412.4 149.0 all-reduce.12
where the time goes:
time: 582 us; the launch traced here: 577 us
  matrix products  232 us (40%)
  waiting for transfers between devices  192 us (33%)
  local copies, waits for them, and re-layouts  87.3 us (15%)
  between operations  35 us (6%)
  other arithmetic  19.4 us (3%)
  starting transfers between devices  10.7 us (2%)
    psum x1, waiting for transfers between devices, shards(): grad_total, weight_total = lax.psum((grad_probe, weight), ('row', 'col'))  149 us
    ppermute x4, waiting for transfers between devices, shifted(): lax.ppermute(value, axis, [(source, source + steps) for source in range(l...  43 us
    dynamic_update_slice x5, local copies, waits for them, and re-layouts, shards(): lax.dynamic_update_slice(grad_ext, previous + grad_windows[slot_index], s...  38.2 us
    dot_general x14, matrix products, product_left(): contract('jk,mkl->mjl', table_real, field_real)  33.3 us
    dot_general x14, matrix products, product_left(): contract('jk,mkl->mjl', table_imag, field_imag)  31.5 us
    dot_general x14, matrix products, product_left(): contract('jk,mkl->mjl', table_imag, field_real)  28.5 us
    dot_general x14, matrix products, product_left(): contract('jk,mkl->mjl', table_real, field_imag)  28.4 us
    dot_general x14, matrix products, product_right(): contract('mjk,kl->mjl', field_real, table_real)  28.2 us
  transfers between devices with their start and end apart: 5, of which 3 were waited for; matrix products, arithmetic and copies ran while one was open for 2% of the time, Pallas kernels for 0%

commit v1 on v0

v1 whole, which is shorter than its diff:
```python
from functools import partial
import math

import jax
import jax.numpy as jnp
import ml_dtypes
import numpy as np
from jax import lax
from jax.experimental import pallas as pl
from jax.experimental.pallas import tpu as pltpu
from jax.sharding import PartitionSpec as P

FRESNEL = 4.0
STEP_OBJECT = 0.5
STEP_PROBE = 0.5
AXES = ("row", "col")
N = 128
MODES = 4
EXT = 384
TILE = 256
VMEM_LIMIT = 50 * 1024 * 1024


def split_np(matrix):
    high = matrix.astype(np.float32).astype(ml_dtypes.bfloat16)
    low = (matrix - high.astype(np.float64)).astype(np.float32).astype(ml_dtypes.bfloat16)
    return np.stack([high, low])


def tables_np():
    position = np.arange(N)
    dft = np.exp(-2j * np.pi * (np.outer(position, position) % N) / N) / math.sqrt(N)
    frequency = np.where(position < N // 2, position, position - N) / N
    chirp = np.exp(-1j * np.pi * FRESNEL * frequency**2)
    propagator = dft.conj() @ (chirp[:, None] * dft)
    propagator = 0.5 * (propagator + propagator.T)
    out = []
    for matrix in (propagator, dft):
        real, imag = matrix.real, matrix.imag
        out.append(
            np.stack(
                [
                    split_np(np.block([[real, imag], [-imag, real]])),
                    split_np(np.block([[real, -imag], [imag, real]])),
                ]
            )
        )
    return np.stack(out)


def split(value):
    high = value.astype(jnp.bfloat16)
    low = (value - high.astype(jnp.float32)).astype(jnp.bfloat16)
    return high, low


def dot(left, right):
    return jnp.dot(left, right, preferred_element_type=jnp.float32)


def mode(value, index):
    return value[index * N : (index + 1) * N]


def sandwich(real, imag, tables, which, conj):
    right_form, left_form = (1, 0) if conj else (0, 1)
    high, low = split(jnp.concatenate([real, imag], axis=1))
    table_high, table_low = tables[which, right_form, 0], tables[which, right_form, 1]
    mixed = dot(high, table_high) + dot(low, table_high) + dot(high, table_low)
    mixed = jnp.concatenate(
        [
            jnp.concatenate([mode(mixed, m)[:, :N] for m in range(MODES)], axis=1),
            jnp.concatenate([mode(mixed, m)[:, N:] for m in range(MODES)], axis=1),
        ],
        axis=0,
    )
    high, low = split(mixed)
    table_high, table_low = tables[which, left_form, 0], tables[which, left_form, 1]
    out = dot(table_high, high) + dot(table_high, low) + dot(table_low, high)
    return (
        jnp.concatenate([out[:N, m * N : (m + 1) * N] for m in range(MODES)], axis=0),
        jnp.concatenate([out[N:, m * N : (m + 1) * N] for m in range(MODES)], axis=0),
    )


def spread(value):
    return jnp.concatenate([value] * MODES, axis=0)


def times(real, imag, other_real, other_imag):
    other_real, other_imag = spread(other_real), spread(other_imag)
    return real * other_real - imag * other_imag, real * other_imag + imag * other_real


def times_conj(real, imag, other_real, other_imag):
    other_real, other_imag = spread(other_real), spread(other_imag)
    return real * other_real + imag * other_imag, imag * other_real - real * other_imag


def sum_modes(value):
    return (mode(value, 0) + mode(value, 1)) + (mode(value, 2) + mode(value, 3))


def slice_gradient(wave_real, wave_imag, grad_real, grad_imag):
    return (
        sum_modes(wave_real * grad_real + wave_imag * grad_imag),
        sum_modes(wave_real * grad_imag - wave_imag * grad_real),
    )


def corner_of(place, slot):
    row, col = place[slot, 0], place[slot, 1]
    tile = jnp.where(col >= N, 1, 0)
    return row, tile, col - tile * N


def cut(ext, part, depth, where):
    row, tile, turn = where
    block = jnp.concatenate([ext[part, depth, tile + k, pl.ds(row, N), :] for k in range(2)], axis=1)
    return pltpu.roll(block, lax.rem(2 * N - turn, 2 * N), 1)[:, :N]


def deposit(ext, part, depth, where, value):
    row, tile, turn = where
    block = pltpu.roll(jnp.concatenate([value, jnp.zeros_like(value)], axis=1), turn, 1)
    for k in range(2):
        ext[part, depth, tile + k, pl.ds(row, N), :] += block[:, k * N : (k + 1) * N]


def run_copies(pairs, sems):
    copies = [pltpu.make_async_copy(*pair, sems.at[k]) for k, pair in enumerate(pairs)]
    for copy in copies:
        copy.start()
    for copy in copies:
        copy.wait()


def load_extended(first, own, bottom, right, corner, ext, sems):
    upper, lower = pl.ds(0, TILE), pl.ds(TILE, N)
    pairs = []
    for k in range(2):
        lanes = pl.ds(k * N, N)
        pairs.append((own.at[:, pl.ds(first, 2), :, lanes], ext.at[:, :, k, upper]))
        pairs.append((bottom.at[:, :, :, lanes], ext.at[:, :, k, lower]))
    pairs.append((right, ext.at[:, :, 2, upper]))
    pairs.append((corner, ext.at[:, :, 2, lower]))
    run_copies(pairs, sems)


def store_gradient(ext, own, bottom, right, sems):
    pairs = []
    for k in range(2):
        lanes = pl.ds(k * N, N)
        pairs.append((ext.at[:, :, k, pl.ds(0, TILE)], own.at[:, :, :, lanes]))
        pairs.append((ext.at[:, :, k, pl.ds(TILE, N)], bottom.at[:, :, :, lanes]))
    pairs.append((ext.at[:, :, 2], right))
    run_copies(pairs, sems)


def first_half(place, count, own, bottom, right, corner, probe, tables, windows, wave1, wave2, weight, ext, sems):
    slot = pl.program_id(0)

    @pl.when(slot == 0)
    def _():
        load_extended(0, own, bottom, right, corner, ext, sems)
        weight[...] = jnp.zeros_like(weight)

    @pl.when(slot < count[0])
    def _():
        where = corner_of(place, slot)
        real, imag = probe[0], probe[1]
        for depth in range(2):
            cut_real, cut_imag = cut(ext, 0, depth, where), cut(ext, 1, depth, where)
            windows[0, 0, depth] = cut_real
            windows[0, 1, depth] = cut_imag
            if depth == 0:
                weight[...] += cut_real * cut_real + cut_imag * cut_imag
            real, imag = sandwich(*times(real, imag, cut_real, cut_imag), tables, 0, False)
            out = (wave1, wave2)[depth]
            out[0, 0] = real
            out[0, 1] = imag


def second_half(
    place, count, own, bottom, right, corner, wave2, amplitude, tables, grad2, grad_own, grad_bottom, grad_right, ext, grad, sems
):
    slot = pl.program_id(0)

    @pl.when(slot == 0)
    def _():
        load_extended(2, own, bottom, right, corner, ext, sems)
        grad[...] = jnp.zeros_like(grad)

    @pl.when(slot < count[0])
    def _():
        where = corner_of(place, slot)
        object2 = cut(ext, 0, 0, where), cut(ext, 1, 0, where)
        object3 = cut(ext, 0, 1, where), cut(ext, 1, 1, where)
        wave3 = sandwich(*times(wave2[0, 0], wave2[0, 1], *object2), tables, 0, False)
        real, imag = sandwich(*times(*wave3, *object3), tables, 1, False)
        scale = jnp.sqrt(sum_modes(real * real + imag * imag) + 1.0)
        factor = spread(2.0 - 2.0 * (amplitude[0] / scale))
        real, imag = sandwich(real * factor, imag * factor, tables, 1, True)
        slice_real, slice_imag = slice_gradient(*wave3, real, imag)
        deposit(grad, 0, 1, where, slice_real)
        deposit(grad, 1, 1, where, slice_imag)
        real, imag = sandwich(*times_conj(real, imag, *object3), tables, 0, True)
        slice_real, slice_imag = slice_gradient(wave2[0, 0], wave2[0, 1], real, imag)
        deposit(grad, 0, 0, where, slice_real)
        deposit(grad, 1, 0, where, slice_imag)
        real, imag = times_conj(real, imag, *object2)
        grad2[0, 0] = real
        grad2[0, 1] = imag

    @pl.when(slot == pl.num_programs(0) - 1)
    def _():
        store_gradient(grad, grad_own, grad_bottom, grad_right, sems)


def third_part(place, count, windows, wave1, grad2, probe, tables, grad_probe, grad_own, grad_bottom, grad_right, grad, sems):
    slot = pl.program_id(0)

    @pl.when(slot == 0)
    def _():
        grad[...] = jnp.zeros_like(grad)
        grad_probe[...] = jnp.zeros_like(grad_probe)

    @pl.when(slot < count[0])
    def _():
        where = corner_of(place, slot)
        real, imag = sandwich(grad2[0, 0], grad2[0, 1], tables, 0, True)
        slice_real, slice_imag = slice_gradient(wave1[0, 0], wave1[0, 1], real, imag)
        deposit(grad, 0, 1, where, slice_real)
        deposit(grad, 1, 1, where, slice_imag)
        real, imag = times_conj(real, imag, windows[0, 0, 1], windows[0, 1, 1])
        real, imag = sandwich(real, imag, tables, 0, True)
        slice_real, slice_imag = slice_gradient(probe[0], probe[1], real, imag)
        deposit(grad, 0, 0, where, slice_real)
        deposit(grad, 1, 0, where, slice_imag)
        real, imag = times_conj(real, imag, windows[0, 0, 0], windows[0, 1, 0])
        grad_probe[0] += real
        grad_probe[1] += imag

    @pl.when(slot == pl.num_programs(0) - 1)
    def _():
        store_gradient(grad, grad_own, grad_bottom, grad_right, sems)


def f32(*shape):
    return jax.ShapeDtypeStruct(shape, jnp.float32)


def whole(*shape):
    return pl.BlockSpec(shape, lambda slot: (0,) * len(shape))


def per_slot(*shape):
    return pl.BlockSpec((1, *shape), lambda slot: (slot,) + (0,) * len(shape))


SMEM = pl.BlockSpec(memory_space=pltpu.SMEM)
HBM = pl.BlockSpec(memory_space=pl.ANY)
PARAMS = pltpu.CompilerParams(vmem_limit_bytes=VMEM_LIMIT, dimension_semantics=("arbitrary",))
TABLES = whole(2, 2, 2, 2 * N, 2 * N)
WAVE = (2, MODES * N, N)
EXTENDED = pltpu.VMEM((2, 2, 3, EXT, N), jnp.float32)


def shifted(value, axis, steps):
    count = lax.axis_size(axis)
    leading, last = (max(0, -steps), min(count, count - steps))
    return lax.ppermute(value, axis, [(source, source + steps) for source in range(leading, last)])


def mesh_perm(move):
    pairs = []
    for z in range(4):
        for x in range(4):
            for y in range(4):
                for core in range(2):
                    to_z, to_x, to_y, to_core = move(z, x, y, core)
                    source = z * 32 + (x * 4 + y) * 2 + core
                    pairs.append((source, to_z * 32 + (to_x * 4 + to_y) * 2 + to_core))
    return pairs


SWAP_CORE = mesh_perm(lambda z, x, y, core: (z, x, y, 1 - core))
ALONG_Z = {k: mesh_perm(lambda z, x, y, core, k=k: (z ^ k, x, y, core)) for k in (1, 2, 3)}
ALONG_X = {k: mesh_perm(lambda z, x, y, core, k=k: (z, x ^ k, y, core)) for k in (1, 2, 3)}
ALONG_Y = {k: mesh_perm(lambda z, x, y, core, k=k: (z, x, y ^ k, core)) for k in (1, 2, 3)}


def probe_update(probe, grad_probe, weight):
    z = lax.axis_index("row")
    core = lax.axis_index("col") % 2
    total = jnp.concatenate([grad_probe.reshape(2 * MODES, N, N), weight[None]], axis=0)
    rows = N // 2

    def part(value, index, size):
        return lax.dynamic_slice_in_dim(value, index * size, size, axis=1)

    total = part(total, core, rows) + lax.ppermute(part(total, 1 - core, rows), AXES, SWAP_CORE)
    rows = rows // 4
    arrived = [lax.ppermute(part(total, z ^ k, rows), AXES, ALONG_Z[k]) for k in (1, 2, 3)]
    total = part(total, z, rows) + arrived[0] + arrived[1] + arrived[2]
    for along in (ALONG_Y, ALONG_X):
        place = lax.axis_index("col") // 2
        place = place % 4 if along is ALONG_Y else place // 4
        arrived = [total] + [lax.ppermute(total, AXES, along[k]) for k in (1, 2, 3)]
        total = (arrived[0] + arrived[1]) + (arrived[2] + arrived[3])
    mine = part(probe.reshape(2 * MODES, N, N), core * 4 + z, rows)
    mine = mine - STEP_PROBE * total[: 2 * MODES] / (total[2 * MODES :] + 1.0)
    arrived = [mine] + [lax.ppermute(mine, AXES, ALONG_Z[k]) for k in (1, 2, 3)]
    half = jnp.zeros((2 * MODES, 4 * rows, N), jnp.float32)
    for k in range(4):
        half = lax.dynamic_update_slice_in_dim(half, arrived[k], (z ^ k) * rows, axis=1)
    other = lax.ppermute(half, AXES, SWAP_CORE)
    low = jnp.where(core == 0, half, other)
    high = jnp.where(core == 0, other, half)
    return jnp.concatenate([low, high], axis=1).reshape(probe.shape)


def shards(tables, object_field, probe, amplitudes, offsets, counts):
    row_index = lax.axis_index("row")
    col_index = lax.axis_index("col")
    slots = offsets.shape[2]
    origin = jnp.stack([row_index * TILE, col_index * TILE]).astype(jnp.int32)
    place = offsets[0, 0] - origin[None, :]
    count = counts[0]
    waves = probe.reshape(WAVE)

    bottoms, rights, corners = [], [], []
    for first in (0, 2):
        piece = object_field[:, first : first + 2]
        bottoms.append(shifted(piece[:, :, :N, :], "row", -1))
        rights.append(shifted(piece[:, :, :, :N], "col", -1))
        corners.append(shifted(bottoms[-1][:, :, :, :N], "col", -1))

    windows, wave1, wave2, weight = pl.pallas_call(
        first_half,
        grid=(slots,),
        in_specs=[SMEM, SMEM, HBM, HBM, HBM, HBM, whole(*WAVE), TABLES],
        out_specs=[per_slot(2, 2, N, N), per_slot(*WAVE), per_slot(*WAVE), whole(N, N)],
        out_shape=[f32(slots, 2, 2, N, N), f32(slots, *WAVE), f32(slots, *WAVE), f32(N, N)],
        scratch_shapes=[EXTENDED, pltpu.SemaphoreType.DMA((6,))],
        compiler_params=PARAMS,
        name="first_half",
    )(place, count, object_field, bottoms[0], rights[0], corners[0], waves, tables)

    grad_specs = [HBM, HBM, HBM]
    grad_shapes = [f32(2, 2, TILE, TILE), f32(2, 2, N, TILE), f32(2, 2, EXT, N)]
    grad2, *late = pl.pallas_call(
        second_half,
        grid=(slots,),
        in_specs=[SMEM, SMEM, HBM, HBM, HBM, HBM, per_slot(*WAVE), per_slot(N, N), TABLES],
        out_specs=[per_slot(*WAVE)] + grad_specs,
        out_shape=[f32(slots, *WAVE)] + grad_shapes,
        scratch_shapes=[EXTENDED, EXTENDED, pltpu.SemaphoreType.DMA((6,))],
        compiler_params=PARAMS,
        name="second_half",
    )(place, count, object_field, bottoms[1], rights[1], corners[1], wave2, amplitudes[0, 0], tables)

    grad_probe, *early = pl.pallas_call(
        third_part,
        grid=(slots,),
        in_specs=[SMEM, SMEM, per_slot(2, 2, N, N), per_slot(*WAVE), per_slot(*WAVE), whole(*WAVE), TABLES],
        out_specs=[whole(*WAVE)] + grad_specs,
        out_shape=[f32(*WAVE)] + grad_shapes,
        scratch_shapes=[EXTENDED, pltpu.SemaphoreType.DMA((5,))],
        compiler_params=PARAMS,
        name="third_part",
    )(place, count, windows, wave1, grad2, waves, tables)

    tiles = []
    for first, (own, bottom, right) in ((0, early), (2, late)):
        returned = shifted(right, "col", 1)
        bottom = bottom.at[:, :, :, :N].add(returned[:, :, TILE:])
        back = shifted(bottom, "row", 1)
        own = own.at[:, :, :, :N].add(returned[:, :, :TILE])
        tiles.append(own.at[:, :, :N, :].add(back))
    new_object = object_field - STEP_OBJECT * jnp.concatenate(tiles, axis=1)
    return new_object, probe_update(probe, grad_probe, weight)


def solution(mesh):
    mapped = jax.shard_map(
        shards,
        mesh=mesh,
        in_specs=(
            P(),
            P(None, None, "row", "col"),
            P(),
            P("row", "col", None, None, None),
            P("row", "col", None, None),
            P("row", "col"),
        ),
        out_specs=(P(None, None, "row", "col"), P()),
        check_vma=False,
    )
    return partial(mapped, jnp.asarray(tables_np()))
```

time: 582 us -> 165 us (0.28)
  matrix products: 232 us -> 0 us
  waiting for transfers between devices: 192 us -> 44.7 us
  local copies, waits for them, and re-layouts: 87.3 us -> 9.08 us
  starting transfers between devices: 10.7 us -> 59.4 us
  Pallas kernels: 0 us -> 38.7 us
  between operations: 35 us -> 1.63 us
  other arithmetic: 19.4 us -> 9.93 us
    dot_general x112 -> x0, matrix products: 232 us -> none  [the longest x14 33.3 us: product_left(): contract('jk,mkl->mjl', table_real, field_real)]
    psum x1 -> x0, waiting for transfers between devices: 149 us -> none  [shards(): grad_total, weight_total = lax.psum((grad_probe, weight), ('row', 'col'))]
    pallas_call x0 -> x3, Pallas kernels: none -> 38.7 us  [the longest x1 18 us: shards(): pl.pallas_call(second_half, grid=(slots,), in_specs=[SMEM, SMEM, HBM, HBM...]
    dynamic_update_slice x5 -> x3, local copies, waits for them, and re-layouts: 38.2 us -> 0.02 us  [probe_update(): lax.dynamic_update_slice_in_dim(half, arrived[k], (z ^ k) * rows, axis=1)]
    ppermute x0 -> x14, starting transfers between devices: none -> 32.5 us  [the longest x3 15.5 us: probe_update(): lax.ppermute(part(total, z ^ k, rows), AXES, ALONG_Z[k])]
    gather x15 -> x0, local copies, waits for them, and re-layouts: 20.9 us -> none
    ppermute x4 -> x10, starting transfers between devices: 10.7 us -> 27 us  [shifted(): lax.ppermute(value, axis, [(source, source + steps) for source in range(l...]
    ppermute x0 -> x14, waiting for transfers between devices: none -> 11.3 us  [the longest x3 3.52 us: probe_update(): lax.ppermute(part(total, z ^ k, rows), AXES, ALONG_Z[k])]
  transfers between devices with their start and end apart: 5 -> 24, of which waited for: 3 -> 14; matrix products, arithmetic and copies ran while one was open for 2% -> 5% of each run, Pallas kernels for 0% -> 6%
where the time goes in v1:
time: 165 us; the launch traced here: 164 us
  starting transfers between devices  59.4 us (36%)
  waiting for transfers between devices  44.7 us (27%)
  Pallas kernels  38.7 us (23%)
  other arithmetic  9.93 us (6%)
  local copies, waits for them, and re-layouts  9.08 us (6%)
    ppermute x10, waiting for transfers between devices, shifted(): lax.ppermute(value, axis, [(source, source + steps) for source in range(l...  33.4 us
    ppermute x10, starting transfers between devices, shifted(): lax.ppermute(value, axis, [(source, source + steps) for source in range(l...  27 us
    pallas_call x1, Pallas kernels, shards(): pl.pallas_call(second_half, grid=(slots,), in_specs=[SMEM, SMEM, HBM, HBM...  18 us
    ppermute x3, starting transfers between devices, probe_update(): lax.ppermute(part(total, z ^ k, rows), AXES, ALONG_Z[k])  15.5 us
    pallas_call x1, Pallas kernels, shards(): pl.pallas_call(first_half, grid=(slots,), in_specs=[SMEM, SMEM, HBM, HBM,...  10.5 us
    pallas_call x1, Pallas kernels, shards(): pl.pallas_call(third_part, grid=(slots,), in_specs=[SMEM, SMEM, per_slot(...  10.2 us
    ppermute x6, starting transfers between devices, probe_update(): arrived = [total] + [lax.ppermute(total, AXES, along[k]) for k in (1, 2, 3)]  8.27 us
    ppermute x3, starting transfers between devices, probe_update(): arrived = [mine] + [lax.ppermute(mine, AXES, ALONG_Z[k]) for k in (1, 2, 3)]  4.02 us
  transfers between devices with their start and end apart: 24, of which 14 were waited for; matrix products, arithmetic and copies ran while one was open for 5% of the time, Pallas kernels for 6%

profile of v1, /device:TPU:1, one launch (start us, length us, event | category | flops | bytes accessed | tf_op | source)
XLA Modules:
  0.0 163.5 jit_solution(11220335053724692542)
XLA Ops:
  0.6 2.4 %fusion.15 = (f32[2,2,128,256]{3,2,1,0:T(8,128)}, f32[2,2,128,256]{3,2,1,0:T(8,128)}) fusion(f32[2,4,256,256]{3,2,1,0:T(8,128)} %own.3), kind=kLoop, calls=%fused_computation.42 | loop fusion | bytes 2097152 | tf_op jit(solution)/shard_map/slice | solution.py:335
  6.8 3.3 %collective-permute-start.1 = (f32[2,2,256,128]{3,2,1,0:T(8,128)}, f32[2,2,256,128]{3,2,1,0:T(8,128)}, u32[]{:S(2)}, u32[]{:S(2)}) collective-permute-start(f32[2,2,256,128]{3,2,1,0:T(8,128)} %get-tuple-element.100), channel_id=1, source_target_pairs={{1,0},{2,1},{3,2},{4,3},{5,4},{6,5},{7,6},{8,7},{9,8},{10,9},{11,1... | collective-permute-start | bytes 1572872 | tf_op jit(solution)/shard_map/ppermute | solution.py:272
  10.2 1.9 %collective-permute-start.4 = (f32[2,2,256,128]{3,2,1,0:T(8,128)}, f32[2,2,256,128]{3,2,1,0:T(8,128)S(1)}, u32[]{:S(2)}, u32[]{:S(2)}) collective-permute-start(f32[2,2,256,128]{3,2,1,0:T(8,128)} %get-tuple-element.101), channel_id=1, source_target_pairs={{1,0},{2,1},{3,2},{4,3},{5,4},{6,5},{7,6},{8,7},{9,8},{10,9},{11,1... | collective-permute-start | bytes 1572872 | tf_op jit(solution)/shard_map/ppermute | solution.py:272
  12.1 7.3 %collective-permute-done.3.bottom = f32[2,2,128,256]{3,2,1,0:T(8,128)S(1)} collective-permute-done((f32[2,2,128,256]{3,2,1,0:T(8,128)}, f32[2,2,128,256]{3,2,1,0:T(8,128)S(1)}, u32[]{:S(2)}, u32[]{:S(2)}) %collective-permute-start.3) | collective-permute-done | bytes 524320 | tf_op jit(solution)/shard_map/ppermute | solution.py:272
  20.1 4.1 %collective-permute-start.5 = (f32[2,2,128,128]{3,2,1,0:T(8,128)}, f32[2,2,128,128]{3,2,1,0:T(8,128)S(1)}, u32[]{:S(2)}, u32[]{:S(2)}) collective-permute-start(f32[2,2,128,128]{3,2,1,0:T(8,128)} %slice.235), channel_id=1, source_target_pairs={{1,0},{2,1},{3,2},{4,3},{5,4},{6,5},{7,6},{8,7},{9,8},{10,9},{11,1... | collective-permute-start | bytes 786440 | tf_op jit(solution)/shard_map/ppermute | solution.py:272
  24.1 6.5 %collective-permute-done.bottom = f32[2,2,128,256]{3,2,1,0:T(8,128)S(1)} collective-permute-done((f32[2,2,128,256]{3,2,1,0:T(8,128)}, f32[2,2,128,256]{3,2,1,0:T(8,128)S(1)}, u32[]{:S(2)}, u32[]{:S(2)}) %collective-permute-start) | collective-permute-done | bytes 524320 | tf_op jit(solution)/shard_map/ppermute | solution.py:272
  31.3 3.2 %collective-permute-start.2 = (f32[2,2,128,128]{3,2,1,0:T(8,128)}, f32[2,2,128,128]{3,2,1,0:T(8,128)}, u32[]{:S(2)}, u32[]{:S(2)}) collective-permute-start(f32[2,2,128,128]{3,2,1,0:T(8,128)} %slice.234), channel_id=1, source_target_pairs={{1,0},{2,1},{3,2},{4,3},{5,4},{6,5},{7,6},{8,7},{9,8},{10,9},{11,1... | collective-permute-start | bytes 786440 | tf_op jit(solution)/shard_map/ppermute | solution.py:272
  35.4 4.7 %collective-permute-done.2.corner = f32[2,2,128,128]{3,2,1,0:T(8,128)} collective-permute-done((f32[2,2,128,128]{3,2,1,0:T(8,128)}, f32[2,2,128,128]{3,2,1,0:T(8,128)}, u32[]{:S(2)}, u32[]{:S(2)}) %collective-permute-start.2) | collective-permute-done | bytes 262176 | tf_op jit(solution)/shard_map/ppermute | solution.py:272
  40.0 10.5 %first_half.1 = (f32[5,2,2,128,128]{4,3,2,1,0:T(8,128)}, f32[5,2,512,128]{3,2,1,0:T(8,128)}, f32[5,2,512,128]{3,2,1,0:T(8,128)}, f32[128,128]{1,0:T(8,128)S(1)}) custom-call(s32[5,2]{1,0:T(8,128)S(1)} %broadcast_subtract_fusion.place, s32[1]{0:T(128)} %bitcast.12.count, f32[2,4,256,256]{3,2,1,0:T(8,128)} %own.3, ...), custom_call_target="tpu_custom_call" | custom-call | tf_op jit(solution)/shard_map/first_half/pallas_call | solution.py:339
  50.6 18.0 %second_half.1 = (f32[5,2,512,128]{3,2,1,0:T(8,128)}, f32[2,2,256,256]{3,2,1,0:T(8,128)S(1)}, f32[2,2,128,256]{3,2,1,0:T(8,128)S(1)}, f32[2,2,384,128]{3,2,1,0:T(8,128)S(1)}) custom-call(s32[5,2]{1,0:T(8,128)S(1)} %broadcast_subtract_fusion.place, s32[1]{0:T(128)} %bitcast.13.count, f32[2,4,256,256]{3,2,1,0:T(8,128)} %own.3, ...), custom_call_target="tpu_custom_call" | custom-call | tf_op jit(solution)/shard_map/second_half/pallas_call | solution.py:352
  70.2 10.2 %third_part.1 = (f32[2,512,128]{2,1,0:T(8,128)S(1)}, f32[2,2,256,256]{3,2,1,0:T(8,128)S(1)}, f32[2,2,128,256]{3,2,1,0:T(8,128)S(1)}, f32[2,2,384,128]{3,2,1,0:T(8,128)S(1)}) custom-call(s32[5,2]{1,0:T(8,128)S(1)} %broadcast_subtract_fusion.place, s32[1]{0:T(128)} %bitcast.14.count, f32[5,2,2,128,128]{4,3,2,1,0:T(8,128)} %get-tuple-element.86.windows, ...), custom_call_target="tpu_custom_call" | custom-call | tf_op jit(solution)/shard_map/third_part/pallas_call | solution.py:363
  86.8 15.5 %collective-permute-start.12 = (f32[9,16,128]{2,1,0:T(8,128)}, f32[9,16,128]{2,1,0:T(8,128)}, u32[]{:S(2)}, u32[]{:S(2)}) collective-permute-start(f32[9,16,128]{2,1,0:T(8,128)} %get-tuple-element.108), channel_id=1, source_target_pairs={{0,64},{1,65},{2,66},{3,67},{4,68},{5,69},{6,70},{7,71},{8,72},{9,... | collective-permute-start | bytes 221192 | tf_op jit(solution)/shard_map/ppermute | solution.py:304
  102.2 2.6 %collective-permute-done.12 = f32[9,16,128]{2,1,0:T(8,128)} collective-permute-done((f32[9,16,128]{2,1,0:T(8,128)}, f32[9,16,128]{2,1,0:T(8,128)}, u32[]{:S(2)}, u32[]{:S(2)}) %collective-permute-start.12) | collective-permute-done | bytes 73760 | tf_op jit(solution)/shard_map/ppermute | solution.py:304
  108.1 2.3 %collective-permute-start.16 = (f32[9,16,128]{2,1,0:T(8,128)S(1)}, f32[9,16,128]{2,1,0:T(8,128)S(1)}, u32[]{:S(2)}, u32[]{:S(2)}) collective-permute-start(f32[9,16,128]{2,1,0:T(8,128)S(1)} %add_add_fusion.2), channel_id=1, source_target_pairs={{0,6},{1,7},{2,4},{3,5},{4,2},{5,3},{6,0},{7,1},{8,14},{9,15},{10,... | collective-permute-start | bytes 221192 | tf_op jit(solution)/shard_map/ppermute | solution.py:309
  114.0 3.7 %collective-permute-start.18 = (f32[9,16,128]{2,1,0:T(8,128)S(1)}, f32[9,16,128]{2,1,0:T(8,128)S(1)}, u32[]{:S(2)}, u32[]{:S(2)}) collective-permute-start(f32[9,16,128]{2,1,0:T(8,128)S(1)} %add_add_fusion.1), channel_id=1, source_target_pairs={{0,16},{1,17},{2,18},{3,19},{4,20},{5,21},{6,22},{7,23},{8,24},{9,... | collective-permute-start | bytes 221192 | tf_op jit(solution)/shard_map/ppermute | solution.py:309
  118.0 5.2 %collective-permute-start.8 = (f32[2,2,384,128]{3,2,1,0:T(8,128)}, f32[2,2,384,128]{3,2,1,0:T(8,128)}, u32[]{:S(2)}, u32[]{:S(2)}) collective-permute-start(f32[2,2,384,128]{3,2,1,0:T(8,128)} %copy-done.7), channel_id=1, source_target_pairs={{0,1},{1,2},{2,3},{3,4},{4,5},{5,6},{6,7},{7,8},{8,9},{9,10},{10,1... | collective-permute-start | bytes 2359304 | tf_op jit(solution)/shard_map/ppermute | solution.py:272
  123.2 1.9 %collective-permute-start.6 = (f32[2,2,384,128]{3,2,1,0:T(8,128)}, f32[2,2,384,128]{3,2,1,0:T(8,128)}, u32[]{:S(2)}, u32[]{:S(2)}) collective-permute-start(f32[2,2,384,128]{3,2,1,0:T(8,128)} %copy-done.6), channel_id=1, source_target_pairs={{0,1},{1,2},{2,3},{3,4},{4,5},{5,6},{6,7},{7,8},{8,9},{9,10},{10,1... | collective-permute-start | bytes 2359304 | tf_op jit(solution)/shard_map/ppermute | solution.py:272
  129.3 2.4 %collective-permute-done.21 = f32[8,16,128]{2,1,0:T(8,128)S(1)} collective-permute-done((f32[8,16,128]{2,1,0:T(8,128)S(1)}, f32[8,16,128]{2,1,0:T(8,128)S(1)}, u32[]{:S(2)}, u32[]{:S(2)}) %collective-permute-start.21) | collective-permute-done | bytes 65568 | tf_op jit(solution)/shard_map/ppermute | solution.py:313
  132.8 3.2 %collective-permute-start.23 = (f32[8,64,128]{2,1,0:T(8,128)S(1)}, f32[8,64,128]{2,1,0:T(8,128)S(1)}, u32[]{:S(2)}, u32[]{:S(2)}) collective-permute-start(f32[8,64,128]{2,1,0:T(8,128)S(1)} %constant_dynamic-update-slice_fusion), channel_id=1, source_target_pairs={{0,1},{1,0},{2,3},{3,2},{4,5},{5,4},{6,7},{7,6},{8,9},{9,8},{10,11... | collective-permute-start | bytes 786440 | tf_op jit(solution)/shard_map/ppermute | solution.py:317
  135.9 1.8 %fusion.8 = f32[2,2,128,256]{3,2,1,0:T(8,128)} fusion(f32[2,2,128,256]{3,2,1,0:T(8,128)} %copy-done.5, f32[2,2,384,128]{3,2,1,0:T(8,128)} %collective-permute-done.8), kind=kLoop, calls=%fused_computation.19 | loop fusion | flops 65536 | bytes 786432 | tf_op jit(solution)/shard_map/scatter-add | solution.py:377
  139.0 1.8 %collective-permute-done.6 = f32[2,2,384,128]{3,2,1,0:T(8,128)} collective-permute-done((f32[2,2,384,128]{3,2,1,0:T(8,128)}, f32[2,2,384,128]{3,2,1,0:T(8,128)}, u32[]{:S(2)}, u32[]{:S(2)}) %collective-permute-start.6) | collective-permute-done | bytes 786464 | tf_op jit(solution)/shard_map/ppermute | solution.py:272
  141.9 3.4 %collective-permute-start.7 = (f32[2,2,128,256]{3,2,1,0:T(8,128)S(1)}, f32[2,2,128,256]{3,2,1,0:T(8,128)S(1)}, u32[]{:S(2)}, u32[]{:S(2)}) collective-permute-start(f32[2,2,128,256]{3,2,1,0:T(8,128)S(1)} %fusion.9), channel_id=1, source_target_pairs={{0,32},{32,64},{64,96},{1,33},{33,65},{65,97},{2,34},{34,66},{66,9... | collective-permute-start | bytes 1572872 | tf_op jit(solution)/shard_map/ppermute | solution.py:272
  148.5 2.2 %collective-permute-done.9 = f32[2,2,128,256]{3,2,1,0:T(8,128)S(1)} collective-permute-done((f32[2,2,128,256]{3,2,1,0:T(8,128)}, f32[2,2,128,256]{3,2,1,0:T(8,128)S(1)}, u32[]{:S(2)}, u32[]{:S(2)}) %collective-permute-start.9) | collective-permute-done | bytes 524320 | tf_op jit(solution)/shard_map/ppermute | solution.py:272
  150.8 11.0 %collective-permute-done.7 = f32[2,2,128,256]{3,2,1,0:T(8,128)S(1)} collective-permute-done((f32[2,2,128,256]{3,2,1,0:T(8,128)S(1)}, f32[2,2,128,256]{3,2,1,0:T(8,128)S(1)}, u32[]{:S(2)}, u32[]{:S(2)}) %collective-permute-start.7) | collective-permute-done | bytes 524320 | tf_op jit(solution)/shard_map/ppermute | solution.py:272
  (77 shorter events, 33.1 us)
Async XLA Ops:
  3.0 16.3 %collective-permute-start.3 = (f32[2,2,128,256]{3,2,1,0:T(8,128)}, f32[2,2,128,256]{3,2,1,0:T(8,128)S(1)}, u32[]{:S(2)}, u32[]{:S(2)}) collective-permute-start(f32[2,2,128,256]{3,2,1,0:T(8,128)} %get-tuple-element.103), channel_id=1, source_target_pairs={{32,0},{64,32},{96,64},{33,1},{65,33},{97,65},{34,2},{66,34},{98,6... | collective-permute-start | bytes 1572872 | tf_op jit(solution)/shard_map/ppermute | solution.py:272
  4.5 26.1 %collective-permute-start = (f32[2,2,128,256]{3,2,1,0:T(8,128)}, f32[2,2,128,256]{3,2,1,0:T(8,128)S(1)}, u32[]{:S(2)}, u32[]{:S(2)}) collective-permute-start(f32[2,2,128,256]{3,2,1,0:T(8,128)} %get-tuple-element.102), channel_id=1, source_target_pairs={{32,0},{64,32},{96,64},{33,1},{65,33},{97,65},{34,2},{66,34},{98,6... | collective-permute-start | bytes 1572872 | tf_op jit(solution)/shard_map/ppermute | solution.py:272
  6.8 28.5 %collective-permute-start.1 = (f32[2,2,256,128]{3,2,1,0:T(8,128)}, f32[2,2,256,128]{3,2,1,0:T(8,128)}, u32[]{:S(2)}, u32[]{:S(2)}) collective-permute-start(f32[2,2,256,128]{3,2,1,0:T(8,128)} %get-tuple-element.100), channel_id=1, source_target_pairs={{1,0},{2,1},{3,2},{4,3},{5,4},{6,5},{7,6},{8,7},{9,8},{10,9},{11,1... | collective-permute-start | bytes 1572872 | tf_op jit(solution)/shard_map/ppermute | solution.py:272
  10.2 40.4 %collective-permute-start.4 = (f32[2,2,256,128]{3,2,1,0:T(8,128)}, f32[2,2,256,128]{3,2,1,0:T(8,128)S(1)}, u32[]{:S(2)}, u32[]{:S(2)}) collective-permute-start(f32[2,2,256,128]{3,2,1,0:T(8,128)} %get-tuple-element.101), channel_id=1, source_target_pairs={{1,0},{2,1},{3,2},{4,3},{5,4},{6,5},{7,6},{8,7},{9,8},{10,9},{11,1... | collective-permute-start | bytes 1572872 | tf_op jit(solution)/shard_map/ppermute | solution.py:272
  20.1 30.5 %collective-permute-start.5 = (f32[2,2,128,128]{3,2,1,0:T(8,128)}, f32[2,2,128,128]{3,2,1,0:T(8,128)S(1)}, u32[]{:S(2)}, u32[]{:S(2)}) collective-permute-start(f32[2,2,128,128]{3,2,1,0:T(8,128)} %slice.235), channel_id=1, source_target_pairs={{1,0},{2,1},{3,2},{4,3},{5,4},{6,5},{7,6},{8,7},{9,8},{10,9},{11,1... | collective-permute-start | bytes 786440 | tf_op jit(solution)/shard_map/ppermute | solution.py:272
  31.3 8.7 %collective-permute-start.2 = (f32[2,2,128,128]{3,2,1,0:T(8,128)}, f32[2,2,128,128]{3,2,1,0:T(8,128)}, u32[]{:S(2)}, u32[]{:S(2)}) collective-permute-start(f32[2,2,128,128]{3,2,1,0:T(8,128)} %slice.234), channel_id=1, source_target_pairs={{1,0},{2,1},{3,2},{4,3},{5,4},{6,5},{7,6},{8,7},{9,8},{10,9},{11,1... | collective-permute-start | bytes 786440 | tf_op jit(solution)/shard_map/ppermute | solution.py:272
  82.2 2.9 %collective-permute-start.10 = (f32[9,64,128]{2,1,0:T(8,128)S(1)}, f32[9,64,128]{2,1,0:T(8,128)}, u32[]{:S(2)}, u32[]{:S(2)}) collective-permute-start(f32[9,64,128]{2,1,0:T(8,128)S(1)} %fusion.5), channel_id=1, source_target_pairs={{0,1},{1,0},{2,3},{3,2},{4,5},{5,4},{6,7},{7,6},{8,9},{9,8},{10,11... | collective-permute-start | bytes 884744 | tf_op jit(solution)/shard_map/ppermute | solution.py:302
  86.8 15.5 %collective-permute-start.13 = (f32[9,16,128]{2,1,0:T(8,128)}, f32[9,16,128]{2,1,0:T(8,128)}, u32[]{:S(2)}, u32[]{:S(2)}) collective-permute-start(f32[9,16,128]{2,1,0:T(8,128)} %get-tuple-element.107), channel_id=1, source_target_pairs={{0,96},{1,97},{2,98},{3,99},{4,100},{5,101},{6,102},{7,103},{8,104... | collective-permute-start | bytes 221192 | tf_op jit(solution)/shard_map/ppermute | solution.py:304
  86.8 18.1 %collective-permute-start.12 = (f32[9,16,128]{2,1,0:T(8,128)}, f32[9,16,128]{2,1,0:T(8,128)}, u32[]{:S(2)}, u32[]{:S(2)}) collective-permute-start(f32[9,16,128]{2,1,0:T(8,128)} %get-tuple-element.108), channel_id=1, source_target_pairs={{0,64},{1,65},{2,66},{3,67},{4,68},{5,69},{6,70},{7,71},{8,72},{9,... | collective-permute-start | bytes 221192 | tf_op jit(solution)/shard_map/ppermute | solution.py:304
  102.2 3.5 %collective-permute-start.11 = (f32[9,16,128]{2,1,0:T(8,128)}, f32[9,16,128]{2,1,0:T(8,128)}, u32[]{:S(2)}, u32[]{:S(2)}) collective-permute-start(f32[9,16,128]{2,1,0:T(8,128)} %get-tuple-element.106), channel_id=1, source_target_pairs={{0,32},{1,33},{2,34},{3,35},{4,36},{5,37},{6,38},{7,39},{8,40},{9,... | collective-permute-start | bytes 221192 | tf_op jit(solution)/shard_map/ppermute | solution.py:304
  106.7 4.8 %collective-permute-start.15 = (f32[9,16,128]{2,1,0:T(8,128)S(1)}, f32[9,16,128]{2,1,0:T(8,128)S(1)}, u32[]{:S(2)}, u32[]{:S(2)}) collective-permute-start(f32[9,16,128]{2,1,0:T(8,128)S(1)} %add_add_fusion.2), channel_id=1, source_target_pairs={{0,4},{1,5},{2,6},{3,7},{4,0},{5,1},{6,2},{7,3},{8,12},{9,13},{10,... | collective-permute-start | bytes 221192 | tf_op jit(solution)/shard_map/ppermute | solution.py:309
  108.1 4.4 %collective-permute-start.16 = (f32[9,16,128]{2,1,0:T(8,128)S(1)}, f32[9,16,128]{2,1,0:T(8,128)S(1)}, u32[]{:S(2)}, u32[]{:S(2)}) collective-permute-start(f32[9,16,128]{2,1,0:T(8,128)S(1)} %add_add_fusion.2), channel_id=1, source_target_pairs={{0,6},{1,7},{2,4},{3,5},{4,2},{5,3},{6,0},{7,1},{8,14},{9,15},{10,... | collective-permute-start | bytes 221192 | tf_op jit(solution)/shard_map/ppermute | solution.py:309
  110.4 3.5 %collective-permute-start.14 = (f32[9,16,128]{2,1,0:T(8,128)S(1)}, f32[9,16,128]{2,1,0:T(8,128)S(1)}, u32[]{:S(2)}, u32[]{:S(2)}) collective-permute-start(f32[9,16,128]{2,1,0:T(8,128)S(1)} %add_add_fusion.2), channel_id=1, source_target_pairs={{0,2},{1,3},{2,0},{3,1},{4,6},{5,7},{6,4},{7,5},{8,10},{9,11},{10,... | collective-permute-start | bytes 221192 | tf_op jit(solution)/shard_map/ppermute | solution.py:309
  114.0 11.2 %collective-permute-start.18 = (f32[9,16,128]{2,1,0:T(8,128)S(1)}, f32[9,16,128]{2,1,0:T(8,128)S(1)}, u32[]{:S(2)}, u32[]{:S(2)}) collective-permute-start(f32[9,16,128]{2,1,0:T(8,128)S(1)} %add_add_fusion.1), channel_id=1, source_target_pairs={{0,16},{1,17},{2,18},{3,19},{4,20},{5,21},{6,22},{7,23},{8,24},{9,... | collective-permute-start | bytes 221192 | tf_op jit(solution)/shard_map/ppermute | solution.py:309
  117.6 7.5 %collective-permute-start.19 = (f32[9,16,128]{2,1,0:T(8,128)S(1)}, f32[9,16,128]{2,1,0:T(8,128)S(1)}, u32[]{:S(2)}, u32[]{:S(2)}) collective-permute-start(f32[9,16,128]{2,1,0:T(8,128)S(1)} %add_add_fusion.1), channel_id=1, source_target_pairs={{0,24},{1,25},{2,26},{3,27},{4,28},{5,29},{6,30},{7,31},{8,16},{9,... | collective-permute-start | bytes 221192 | tf_op jit(solution)/shard_map/ppermute | solution.py:309
  118.0 7.1 %collective-permute-start.17 = (f32[9,16,128]{2,1,0:T(8,128)S(1)}, f32[9,16,128]{2,1,0:T(8,128)S(1)}, u32[]{:S(2)}, u32[]{:S(2)}) collective-permute-start(f32[9,16,128]{2,1,0:T(8,128)S(1)} %add_add_fusion.1), channel_id=1, source_target_pairs={{0,8},{1,9},{2,10},{3,11},{4,12},{5,13},{6,14},{7,15},{8,0},{9,1},... | collective-permute-start | bytes 221192 | tf_op jit(solution)/shard_map/ppermute | solution.py:309
  118.0 17.9 %collective-permute-start.8 = (f32[2,2,384,128]{3,2,1,0:T(8,128)}, f32[2,2,384,128]{3,2,1,0:T(8,128)}, u32[]{:S(2)}, u32[]{:S(2)}) collective-permute-start(f32[2,2,384,128]{3,2,1,0:T(8,128)} %copy-done.7), channel_id=1, source_target_pairs={{0,1},{1,2},{2,3},{3,4},{4,5},{5,6},{6,7},{7,8},{8,9},{9,10},{10,1... | collective-permute-start | bytes 2359304 | tf_op jit(solution)/shard_map/ppermute | solution.py:272
  123.2 17.7 %collective-permute-start.6 = (f32[2,2,384,128]{3,2,1,0:T(8,128)}, f32[2,2,384,128]{3,2,1,0:T(8,128)}, u32[]{:S(2)}, u32[]{:S(2)}) collective-permute-start(f32[2,2,384,128]{3,2,1,0:T(8,128)} %copy-done.6), channel_id=1, source_target_pairs={{0,1},{1,2},{2,3},{3,4},{4,5},{5,6},{6,7},{7,8},{8,9},{9,10},{10,1... | collective-permute-start | bytes 2359304 | tf_op jit(solution)/shard_map/ppermute | solution.py:272
  125.3 4.0 %collective-permute-start.20 = (f32[8,16,128]{2,1,0:T(8,128)S(1)}, f32[8,16,128]{2,1,0:T(8,128)S(1)}, u32[]{:S(2)}, u32[]{:S(2)}) collective-permute-start(f32[8,16,128]{2,1,0:T(8,128)S(1)} %get-tuple-element.99), channel_id=1, source_target_pairs={{0,32},{1,33},{2,34},{3,35},{4,36},{5,37},{6,38},{7,39},{8,40},{9,... | collective-permute-start | bytes 196616 | tf_op jit(solution)/shard_map/ppermute | solution.py:313
  126.8 4.9 %collective-permute-start.21 = (f32[8,16,128]{2,1,0:T(8,128)S(1)}, f32[8,16,128]{2,1,0:T(8,128)S(1)}, u32[]{:S(2)}, u32[]{:S(2)}) collective-permute-start(f32[8,16,128]{2,1,0:T(8,128)S(1)} %get-tuple-element.99), channel_id=1, source_target_pairs={{0,64},{1,65},{2,66},{3,67},{4,68},{5,69},{6,70},{7,71},{8,72},{9,... | collective-permute-start | bytes 196616 | tf_op jit(solution)/shard_map/ppermute | solution.py:313
  128.4 4.3 %collective-permute-start.22 = (f32[8,16,128]{2,1,0:T(8,128)S(1)}, f32[8,16,128]{2,1,0:T(8,128)S(1)}, u32[]{:S(2)}, u32[]{:S(2)}) collective-permute-start(f32[8,16,128]{2,1,0:T(8,128)S(1)} %get-tuple-element.99), channel_id=1, source_target_pairs={{0,96},{1,97},{2,98},{3,99},{4,100},{5,101},{6,102},{7,103},{8,104... | collective-permute-start | bytes 196616 | tf_op jit(solution)/shard_map/ppermute | solution.py:313
  132.8 14.8 %collective-permute-start.23 = (f32[8,64,128]{2,1,0:T(8,128)S(1)}, f32[8,64,128]{2,1,0:T(8,128)S(1)}, u32[]{:S(2)}, u32[]{:S(2)}) collective-permute-start(f32[8,64,128]{2,1,0:T(8,128)S(1)} %constant_dynamic-update-slice_fusion), channel_id=1, source_target_pairs={{0,1},{1,0},{2,3},{3,2},{4,5},{5,4},{6,7},{7,6},{8,9},{9,8},{10,11... | collective-permute-start | bytes 786440 | tf_op jit(solution)/shard_map/ppermute | solution.py:317
  137.7 12.9 %collective-permute-start.9 = (f32[2,2,128,256]{3,2,1,0:T(8,128)}, f32[2,2,128,256]{3,2,1,0:T(8,128)S(1)}, u32[]{:S(2)}, u32[]{:S(2)}) collective-permute-start(f32[2,2,128,256]{3,2,1,0:T(8,128)} %fusion.8), channel_id=1, source_target_pairs={{0,32},{32,64},{64,96},{1,33},{33,65},{65,97},{2,34},{34,66},{66,9... | collective-permute-start | bytes 1572872 | tf_op jit(solution)/shard_map/ppermute | solution.py:272
  141.9 19.9 %collective-permute-start.7 = (f32[2,2,128,256]{3,2,1,0:T(8,128)S(1)}, f32[2,2,128,256]{3,2,1,0:T(8,128)S(1)}, u32[]{:S(2)}, u32[]{:S(2)}) collective-permute-start(f32[2,2,128,256]{3,2,1,0:T(8,128)S(1)} %fusion.9), channel_id=1, source_target_pairs={{0,32},{32,64},{64,96},{1,33},{33,65},{65,97},{2,34},{34,66},{66,9... | collective-permute-start | bytes 1572872 | tf_op jit(solution)/shard_map/ppermute | solution.py:272
  (11 other events, 193.6 us)

commit v2 on v1

--- a/solution.py
+++ b/solution.py
@@ -58,53 +58,63 @@
     return jnp.dot(left, right, preferred_element_type=jnp.float32)
 
 
-def mode(value, index):
-    return value[index * N : (index + 1) * N]
-
-
-def sandwich(real, imag, tables, which, conj):
+def sandwich(waves, tables, which, conj):
     right_form, left_form = (1, 0) if conj else (0, 1)
-    high, low = split(jnp.concatenate([real, imag], axis=1))
-    table_high, table_low = tables[which, right_form, 0], tables[which, right_form, 1]
-    mixed = dot(high, table_high) + dot(low, table_high) + dot(high, table_low)
-    mixed = jnp.concatenate(
-        [
-            jnp.concatenate([mode(mixed, m)[:, :N] for m in range(MODES)], axis=1),
-            jnp.concatenate([mode(mixed, m)[:, N:] for m in range(MODES)], axis=1),
-        ],
-        axis=0,
-    )
-    high, low = split(mixed)
-    table_high, table_low = tables[which, left_form, 0], tables[which, left_form, 1]
-    out = dot(table_high, high) + dot(table_high, low) + dot(table_low, high)
+    high, low = tables[which, right_form, 0], tables[which, right_form, 1]
+    right = jnp.concatenate([high, high, low], axis=0)
+    high, low = tables[which, left_form, 0], tables[which, left_form, 1]
+    left = jnp.concatenate([high, high, low], axis=1)
+    mixed = []
+    for wave in waves:
+        high, low = split(jnp.concatenate(wave, axis=1))
+        mixed.append(dot(jnp.concatenate([high, low, high], axis=1), right))
+    out = []
+    for first in range(0, MODES, 2):
+        pair = mixed[first : first + 2]
+        high, low = split(
+            jnp.concatenate(
+                [
+                    jnp.concatenate([wave[:, :N] for wave in pair], axis=1),
+                    jnp.concatenate([wave[:, N:] for wave in pair], axis=1),
+                ],
+                axis=0,
+            )
+        )
+        operand = jnp.concatenate([high, low, high], axis=0)
+        real, imag = dot(left[:N], operand), dot(left[N:], operand)
+        out += [(real[:, :N], imag[:, :N]), (real[:, N:], imag[:, N:])]
+    return out
+
+
+def load_waves(ref):
+    return [(ref[0, m * N : (m + 1) * N], ref[1, m * N : (m + 1) * N]) for m in range(MODES)]
+
+
+def store_waves(ref, waves):
+    for m, (real, imag) in enumerate(waves):
+        ref[0, m * N : (m + 1) * N] = real
+        ref[1, m * N : (m + 1) * N] = imag
+
+
+def times(waves, other):
+    a, b = other
+    return [(real * a - imag * b, real * b + imag * a) for real, imag in waves]
+
+
+def times_conj(waves, other):
+    a, b = other
+    return [(real * a + imag * b, imag * a - real * b) for real, imag in waves]
+
+
+def sum_modes(terms):
+    return (terms[0] + terms[1]) + (terms[2] + terms[3])
+
+
+def slice_gradient(waves, grads):
+    pairs = [(*wave, *grad) for wave, grad in zip(waves, grads)]
     return (
-        jnp.concatenate([out[:N, m * N : (m + 1) * N] for m in range(MODES)], axis=0),
-        jnp.concatenate([out[N:, m * N : (m + 1) * N] for m in range(MODES)], axis=0),
-    )
-
-
-def spread(value):
-    return jnp.concatenate([value] * MODES, axis=0)
-
-
-def times(real, imag, other_real, other_imag):
-    other_real, other_imag = spread(other_real), spread(other_imag)
-    return real * other_real - imag * other_imag, real * other_imag + imag * other_real
-
-
-def times_conj(real, imag, other_real, other_imag):
-    other_real, other_imag = spread(other_real), spread(other_imag)
-    return real * other_real + imag * other_imag, imag * other_real - real * other_imag
-
-
-def sum_modes(value):
-    return (mode(value, 0) + mode(value, 1)) + (mode(value, 2) + mode(value, 3))
-
-
-def slice_gradient(wave_real, wave_imag, grad_real, grad_imag):
-    return (
-        sum_modes(wave_real * grad_real + wave_imag * grad_imag),
-        sum_modes(wave_real * grad_imag - wave_imag * grad_real),
+        sum_modes([a * c + b * d for a, b, c, d in pairs]),
+        sum_modes([a * d - b * c for a, b, c, d in pairs]),
     )
 
 
@@ -157,6 +167,15 @@
     run_copies(pairs, sems)
 
 
+def cut_slice(ext, depth, where):
+    return cut(ext, 0, depth, where), cut(ext, 1, depth, where)
+
+
+def deposit_slice(grad, depth, where, value):
+    deposit(grad, 0, depth, where, value[0])
+    deposit(grad, 1, depth, where, value[1])
+
+
 def first_half(place, count, own, bottom, right, corner, probe, tables, windows, wave1, wave2, weight, ext, sems):
     slot = pl.program_id(0)
 
@@ -168,21 +187,18 @@
     @pl.when(slot < count[0])
     def _():
         where = corner_of(place, slot)
-        real, imag = probe[0], probe[1]
+        waves = load_waves(probe)
         for depth in range(2):
-            cut_real, cut_imag = cut(ext, 0, depth, where), cut(ext, 1, depth, where)
-            windows[0, 0, depth] = cut_real
-            windows[0, 1, depth] = cut_imag
+            window = cut_slice(ext, depth, where)
+            windows[0, 0, depth], windows[0, 1, depth] = window
             if depth == 0:
-                weight[...] += cut_real * cut_real + cut_imag * cut_imag
-            real, imag = sandwich(*times(real, imag, cut_real, cut_imag), tables, 0, False)
-            out = (wave1, wave2)[depth]
-            out[0, 0] = real
-            out[0, 1] = imag
+                weight[...] += window[0] * window[0] + window[1] * window[1]
+            waves = sandwich(times(waves, window), tables, 0, False)
+            store_waves((wave1, wave2)[depth].at[0], waves)
 
 
 def second_half(
-    place, count, own, bottom, right, corner, wave2, amplitude, tables, grad2, grad_own, grad_bottom, grad_right, ext, grad, sems
+    place, count, own, bottom, right, corner, wave2, amplitude, tables, grad2, grad_own, grad_bottom, grad_right, ext, grad, wave3, sems
 ):
     slot = pl.program_id(0)
 
@@ -194,23 +210,17 @@
     @pl.when(slot < count[0])
     def _():
         where = corner_of(place, slot)
-        object2 = cut(ext, 0, 0, where), cut(ext, 1, 0, where)
-        object3 = cut(ext, 0, 1, where), cut(ext, 1, 1, where)
-        wave3 = sandwich(*times(wave2[0, 0], wave2[0, 1], *object2), tables, 0, False)
-        real, imag = sandwich(*times(*wave3, *object3), tables, 1, False)
-        scale = jnp.sqrt(sum_modes(real * real + imag * imag) + 1.0)
-        factor = spread(2.0 - 2.0 * (amplitude[0] / scale))
-        real, imag = sandwich(real * factor, imag * factor, tables, 1, True)
-        slice_real, slice_imag = slice_gradient(*wave3, real, imag)
-        deposit(grad, 0, 1, where, slice_real)
-        deposit(grad, 1, 1, where, slice_imag)
-        real, imag = sandwich(*times_conj(real, imag, *object3), tables, 0, True)
-        slice_real, slice_imag = slice_gradient(wave2[0, 0], wave2[0, 1], real, imag)
-        deposit(grad, 0, 0, where, slice_real)
-        deposit(grad, 1, 0, where, slice_imag)
-        real, imag = times_conj(real, imag, *object2)
-        grad2[0, 0] = real
-        grad2[0, 1] = imag
+        object2, object3 = cut_slice(ext, 0, where), cut_slice(ext, 1, where)
+        waves = sandwich(times(load_waves(wave2.at[0]), object2), tables, 0, False)
+        store_waves(wave3, waves)
+        far = sandwich(times(waves, object3), tables, 1, False)
+        intensity = sum_modes([real * real + imag * imag for real, imag in far])
+        factor = 2.0 - 2.0 * (amplitude[0] / jnp.sqrt(intensity + 1.0))
+        grads = sandwich([(real * factor, imag * factor) for real, imag in far], tables, 1, True)
+        deposit_slice(grad, 1, where, slice_gradient(load_waves(wave3), grads))
+        grads = sandwich(times_conj(grads, object3), tables, 0, True)
+        deposit_slice(grad, 0, where, slice_gradient(load_waves(wave2.at[0]), grads))
+        store_waves(grad2.at[0], times_conj(grads, object2))
 
     @pl.when(slot == pl.num_programs(0) - 1)
     def _():
@@ -228,22 +238,23 @@
     @pl.when(slot < count[0])
     def _():
         where = corner_of(place, slot)
-        real, imag = sandwich(grad2[0, 0], grad2[0, 1], tables, 0, True)
-        slice_real, slice_imag = slice_gradient(wave1[0, 0], wave1[0, 1], real, imag)
-        deposit(grad, 0, 1, where, slice_real)
-        deposit(grad, 1, 1, where, slice_imag)
-        real, imag = times_conj(real, imag, windows[0, 0, 1], windows[0, 1, 1])
-        real, imag = sandwich(real, imag, tables, 0, True)
-        slice_real, slice_imag = slice_gradient(probe[0], probe[1], real, imag)
-        deposit(grad, 0, 0, where, slice_real)
-        deposit(grad, 1, 0, where, slice_imag)
-        real, imag = times_conj(real, imag, windows[0, 0, 0], windows[0, 1, 0])
-        grad_probe[0] += real
-        grad_probe[1] += imag
+        object0, object1 = [(windows[0, 0, depth], windows[0, 1, depth]) for depth in range(2)]
+        grads = sandwich(load_waves(grad2.at[0]), tables, 0, True)
+        deposit_slice(grad, 1, where, slice_gradient(load_waves(wave1.at[0]), grads))
+        grads = sandwich(times_conj(grads, object1), tables, 0, True)
+        deposit_slice(grad, 0, where, slice_gradient(load_waves(probe), grads))
+        for m, (real, imag) in enumerate(times_conj(grads, object0)):
+            grad_probe[0, m * N : (m + 1) * N] += real
+            grad_probe[1, m * N : (m + 1) * N] += imag
 
     @pl.when(slot == pl.num_programs(0) - 1)
     def _():
         store_gradient(grad, grad_own, grad_bottom, grad_right, sems)
+
+
+def cost(products):
+    flops = products * 5 * 3 * 2 * MODES * N * (2 * N) * (2 * N)
+    return pl.CostEstimate(flops=2 * flops, bytes_accessed=8 * 2**20, transcendentals=0)
 
 
 def f32(*shape):
@@ -290,34 +301,48 @@
 ALONG_Y = {k: mesh_perm(lambda z, x, y, core, k=k: (z, x, y ^ k, core)) for k in (1, 2, 3)}
 
 
-def probe_update(probe, grad_probe, weight):
+QUARTER = N // 8
+
+
+def part(value, index, size):
+    return lax.dynamic_slice_in_dim(value, index * size, size, axis=1)
+
+
+def share_of_sum(grad_probe, weight):
     z = lax.axis_index("row")
     core = lax.axis_index("col") % 2
     total = jnp.concatenate([grad_probe.reshape(2 * MODES, N, N), weight[None]], axis=0)
     rows = N // 2
-
-    def part(value, index, size):
-        return lax.dynamic_slice_in_dim(value, index * size, size, axis=1)
-
     total = part(total, core, rows) + lax.ppermute(part(total, 1 - core, rows), AXES, SWAP_CORE)
-    rows = rows // 4
-    arrived = [lax.ppermute(part(total, z ^ k, rows), AXES, ALONG_Z[k]) for k in (1, 2, 3)]
-    total = part(total, z, rows) + arrived[0] + arrived[1] + arrived[2]
+    arrived = [lax.ppermute(part(total, z ^ k, QUARTER), AXES, ALONG_Z[k]) for k in (1, 2, 3)]
+    return part(total, z, QUARTER) + arrived[0] + arrived[1] + arrived[2]
+
+
+def sum_plane(total):
     for along in (ALONG_Y, ALONG_X):
-        place = lax.axis_index("col") // 2
-        place = place % 4 if along is ALONG_Y else place // 4
         arrived = [total] + [lax.ppermute(total, AXES, along[k]) for k in (1, 2, 3)]
         total = (arrived[0] + arrived[1]) + (arrived[2] + arrived[3])
-    mine = part(probe.reshape(2 * MODES, N, N), core * 4 + z, rows)
+    return total
+
+
+def gather_half(probe, total):
+    z = lax.axis_index("row")
+    core = lax.axis_index("col") % 2
+    mine = part(probe.reshape(2 * MODES, N, N), core * 4 + z, QUARTER)
     mine = mine - STEP_PROBE * total[: 2 * MODES] / (total[2 * MODES :] + 1.0)
     arrived = [mine] + [lax.ppermute(mine, AXES, ALONG_Z[k]) for k in (1, 2, 3)]
-    half = jnp.zeros((2 * MODES, 4 * rows, N), jnp.float32)
+    half = jnp.zeros((2 * MODES, N // 2, N), jnp.float32)
     for k in range(4):
-        half = lax.dynamic_update_slice_in_dim(half, arrived[k], (z ^ k) * rows, axis=1)
+        half = lax.dynamic_update_slice_in_dim(half, arrived[k], (z ^ k) * QUARTER, axis=1)
+    return half
+
+
+def gather_whole(half):
+    core = lax.axis_index("col") % 2
     other = lax.ppermute(half, AXES, SWAP_CORE)
     low = jnp.where(core == 0, half, other)
     high = jnp.where(core == 0, other, half)
-    return jnp.concatenate([low, high], axis=1).reshape(probe.shape)
+    return jnp.concatenate([low, high], axis=1)
 
 
 def shards(tables, object_field, probe, amplitudes, offsets, counts):
@@ -344,6 +369,7 @@
         out_shape=[f32(slots, 2, 2, N, N), f32(slots, *WAVE), f32(slots, *WAVE), f32(N, N)],
         scratch_shapes=[EXTENDED, pltpu.SemaphoreType.DMA((6,))],
         compiler_params=PARAMS,
+        cost_estimate=cost(4),
         name="first_half",
     )(place, count, object_field, bottoms[0], rights[0], corners[0], waves, tables)
 
@@ -355,8 +381,9 @@
         in_specs=[SMEM, SMEM, HBM, HBM, HBM, HBM, per_slot(*WAVE), per_slot(N, N), TABLES],
         out_specs=[per_slot(*WAVE)] + grad_specs,
         out_shape=[f32(slots, *WAVE)] + grad_shapes,
-        scratch_shapes=[EXTENDED, EXTENDED, pltpu.SemaphoreType.DMA((6,))],
+        scratch_shapes=[EXTENDED, EXTENDED, pltpu.VMEM(WAVE, jnp.float32), pltpu.SemaphoreType.DMA((6,))],
         compiler_params=PARAMS,
+        cost_estimate=cost(8),
         name="second_half",
     )(place, count, object_field, bottoms[1], rights[1], corners[1], wave2, amplitudes[0, 0], tables)
 
@@ -368,18 +395,26 @@
         out_shape=[f32(*WAVE)] + grad_shapes,
         scratch_shapes=[EXTENDED, pltpu.SemaphoreType.DMA((5,))],
         compiler_params=PARAMS,
+        cost_estimate=cost(4),
         name="third_part",
     )(place, count, windows, wave1, grad2, waves, tables)
 
+    returned_late = shifted(late[2], "col", 1)
+    grad_probe, returned_late = lax.optimization_barrier((grad_probe, returned_late))
+    back_late = shifted(late[1].at[:, :, :, :N].add(returned_late[:, :, TILE:]), "row", 1)
+    returned_early = shifted(early[2], "col", 1)
+    quarter = share_of_sum(grad_probe, weight)
+    quarter, returned_early = lax.optimization_barrier((quarter, returned_early))
+    back_early = shifted(early[1].at[:, :, :, :N].add(returned_early[:, :, TILE:]), "row", 1)
+    quarter, back_late = lax.optimization_barrier((sum_plane(quarter), back_late))
+    half = gather_half(probe, quarter)
+    half, back_early = lax.optimization_barrier((half, back_early))
     tiles = []
-    for first, (own, bottom, right) in ((0, early), (2, late)):
-        returned = shifted(right, "col", 1)
-        bottom = bottom.at[:, :, :, :N].add(returned[:, :, TILE:])
-        back = shifted(bottom, "row", 1)
+    for own, returned, back in ((early[0], returned_early, back_early), (late[0], returned_late, back_late)):
         own = own.at[:, :, :, :N].add(returned[:, :, :TILE])
         tiles.append(own.at[:, :, :N, :].add(back))
     new_object = object_field - STEP_OBJECT * jnp.concatenate(tiles, axis=1)
-    return new_object, probe_update(probe, grad_probe, weight)
+    return new_object, gather_whole(half).reshape(probe.shape)
 
 
 def solution(mesh):

time: 165 us -> 125 us (0.76)
  waiting for transfers between devices: 44.7 us -> 23.9 us
  starting transfers between devices: 59.4 us -> 46.8 us
  other arithmetic: 9.93 us -> 7.22 us
  Pallas kernels: 38.7 us -> 36.4 us
  local copies, waits for them, and re-layouts: 9.08 us -> 7.11 us
    ppermute x10, waiting for transfers between devices: 33.4 us -> 12.9 us  [shifted(): lax.ppermute(value, axis, [(source, source + steps) for source in range(l...]
    ppermute x14, starting transfers between devices: 32.5 us -> 19.1 us  [the longest x6 9.17 us: sum_plane(): arrived = [total] + [lax.ppermute(total, AXES, along[k]) for k in (1, 2, 3)]]
    scatter-add x2, other arithmetic: 2.79 us -> 1.07 us  [the longest x1 1.01 us: shards(): late[1].at[:, :, :, :N].add(returned_late[:, :, TILE:])]
    unnamed x22 -> x20, local copies, waits for them, and re-layouts: 3.36 us -> 2.74 us
  transfers between devices with their start and end apart: 24 -> 24, of which waited for: 14 -> 6; matrix products, arithmetic and copies ran while one was open for 5% -> 7% of each run, Pallas kernels for 6% -> 15%
where the time goes in v2:
time: 125 us; the launch traced here: 123 us
  starting transfers between devices  46.8 us (37%)
  Pallas kernels  36.4 us (29%)
  waiting for transfers between devices  23.9 us (19%)
  other arithmetic  7.22 us (6%)
  local copies, waits for them, and re-layouts  7.11 us (6%)
  between operations  1.78 us (1%)
    ppermute x10, starting transfers between devices, shifted(): lax.ppermute(value, axis, [(source, source + steps) for source in range(l...  27.7 us
    pallas_call x1, Pallas kernels, shards(): pl.pallas_call(second_half, grid=(slots,), in_specs=[SMEM, SMEM, HBM, HBM...  17.9 us
    ppermute x10, waiting for transfers between devices, shifted(): lax.ppermute(value, axis, [(source, source + steps) for source in range(l...  12.9 us
    pallas_call x1, Pallas kernels, shards(): pl.pallas_call(first_half, grid=(slots,), in_specs=[SMEM, SMEM, HBM, HBM,...  9.35 us
    ppermute x6, starting transfers between devices, sum_plane(): arrived = [total] + [lax.ppermute(total, AXES, along[k]) for k in (1, 2, 3)]  9.17 us
    pallas_call x1, Pallas kernels, shards(): pl.pallas_call(third_part, grid=(slots,), in_specs=[SMEM, SMEM, per_slot(...  9.15 us
    ppermute x3, waiting for transfers between devices, gather_half(): arrived = [mine] + [lax.ppermute(mine, AXES, ALONG_Z[k]) for k in (1, 2, 3)]  7.81 us
    ppermute x3, starting transfers between devices, gather_half(): arrived = [mine] + [lax.ppermute(mine, AXES, ALONG_Z[k]) for k in (1, 2, 3)]  3.94 us
  transfers between devices with their start and end apart: 24, of which 6 were waited for; matrix products, arithmetic and copies ran while one was open for 7% of the time, Pallas kernels for 15%

profile of v2, /device:TPU:1, one launch (start us, length us, event | category | flops | bytes accessed | tf_op | source)
XLA Modules:
  0.0 123.2 jit_solution(4987593245956600286)
XLA Ops:
  0.7 2.4 %fusion.7 = (f32[2,2,128,256]{3,2,1,0:T(8,128)}, f32[2,2,128,256]{3,2,1,0:T(8,128)}) fusion(f32[2,4,256,256]{3,2,1,0:T(8,128)} %own.3), kind=kLoop, calls=%fused_computation.35 | loop fusion | bytes 2097152 | tf_op jit(solution)/shard_map/slice | solution.py:360
  6.9 3.3 %collective-permute-start.1 = (f32[2,2,256,128]{3,2,1,0:T(8,128)}, f32[2,2,256,128]{3,2,1,0:T(8,128)S(1)}, u32[]{:S(2)}, u32[]{:S(2)}) collective-permute-start(f32[2,2,256,128]{3,2,1,0:T(8,128)} %get-tuple-element.116), channel_id=1, source_target_pairs={{1,0},{2,1},{3,2},{4,3},{5,4},{6,5},{7,6},{8,7},{9,8},{10,9},{11,1... | collective-permute-start | bytes 1572872 | tf_op jit(solution)/shard_map/ppermute | solution.py:283
  10.2 1.9 %collective-permute-start.4 = (f32[2,2,256,128]{3,2,1,0:T(8,128)}, f32[2,2,256,128]{3,2,1,0:T(8,128)}, u32[]{:S(2)}, u32[]{:S(2)}) collective-permute-start(f32[2,2,256,128]{3,2,1,0:T(8,128)} %get-tuple-element.117), channel_id=1, source_target_pairs={{1,0},{2,1},{3,2},{4,3},{5,4},{6,5},{7,6},{8,7},{9,8},{10,9},{11,1... | collective-permute-start | bytes 1572872 | tf_op jit(solution)/shard_map/ppermute | solution.py:283
  12.1 7.2 %collective-permute-done.bottom = f32[2,2,128,256]{3,2,1,0:T(8,128)S(1)} collective-permute-done((f32[2,2,128,256]{3,2,1,0:T(8,128)}, f32[2,2,128,256]{3,2,1,0:T(8,128)S(1)}, u32[]{:S(2)}, u32[]{:S(2)}) %collective-permute-start) | collective-permute-done | bytes 524320 | tf_op jit(solution)/shard_map/ppermute | solution.py:283
  20.1 4.1 %collective-permute-start.2 = (f32[2,2,128,128]{3,2,1,0:T(8,128)}, f32[2,2,128,128]{3,2,1,0:T(8,128)S(1)}, u32[]{:S(2)}, u32[]{:S(2)}) collective-permute-start(f32[2,2,128,128]{3,2,1,0:T(8,128)} %slice.234), channel_id=1, source_target_pairs={{1,0},{2,1},{3,2},{4,3},{5,4},{6,5},{7,6},{8,7},{9,8},{10,9},{11,1... | collective-permute-start | bytes 786440 | tf_op jit(solution)/shard_map/ppermute | solution.py:283
  25.0 5.6 %collective-permute-done.3.bottom = f32[2,2,128,256]{3,2,1,0:T(8,128)S(1)} collective-permute-done((f32[2,2,128,256]{3,2,1,0:T(8,128)}, f32[2,2,128,256]{3,2,1,0:T(8,128)S(1)}, u32[]{:S(2)}, u32[]{:S(2)}) %collective-permute-start.3) | collective-permute-done | bytes 524320 | tf_op jit(solution)/shard_map/ppermute | solution.py:283
  30.6 3.2 %collective-permute-start.5 = (f32[2,2,128,128]{3,2,1,0:T(8,128)S(1)}, f32[2,2,128,128]{3,2,1,0:T(8,128)S(1)}, u32[]{:S(2)}, u32[]{:S(2)}) collective-permute-start(f32[2,2,128,128]{3,2,1,0:T(8,128)S(1)} %slice.235), channel_id=1, source_target_pairs={{1,0},{2,1},{3,2},{4,3},{5,4},{6,5},{7,6},{8,7},{9,8},{10,9},{11,1... | collective-permute-start | bytes 786440 | tf_op jit(solution)/shard_map/ppermute | solution.py:283
  33.8 9.3 %first_half.1 = (f32[5,2,2,128,128]{4,3,2,1,0:T(8,128)}, f32[5,2,512,128]{3,2,1,0:T(8,128)}, f32[5,2,512,128]{3,2,1,0:T(8,128)}, f32[128,128]{1,0:T(8,128)S(1)}) custom-call(s32[5,2]{1,0:T(8,128)S(1)} %broadcast_subtract_fusion.place, s32[1]{0:T(128)} %bitcast.12.count, f32[2,4,256,256]{3,2,1,0:T(8,128)} %own.3, ...), custom_call_target="tpu_custom_call" | custom-call | flops 8053063680 | bytes 8388608 | tf_op jit(solution)/shard_map/first_half/pallas_call | solution.py:364
  43.2 17.9 %second_half.1 = (f32[5,2,512,128]{3,2,1,0:T(8,128)}, f32[2,2,256,256]{3,2,1,0:T(8,128)S(1)}, f32[2,2,128,256]{3,2,1,0:T(8,128)S(1)}, f32[2,2,384,128]{3,2,1,0:T(8,128)}) custom-call(s32[5,2]{1,0:T(8,128)S(1)} %broadcast_subtract_fusion.place, s32[1]{0:T(128)} %bitcast.13.count, f32[2,4,256,256]{3,2,1,0:T(8,128)} %own.3, ...), custom_call_target="tpu_custom_call" | custom-call | flops 16106127360 | bytes 8388608 | tf_op jit(solution)/shard_map/second_half/pallas_call | solution.py:378
  62.0 1.9 %collective-permute-start.6 = (f32[2,2,384,128]{3,2,1,0:T(8,128)}, f32[2,2,384,128]{3,2,1,0:T(8,128)}, u32[]{:S(2)}, u32[]{:S(2)}) collective-permute-start(f32[2,2,384,128]{3,2,1,0:T(8,128)} %get-tuple-element.100), channel_id=1, source_target_pairs={{0,1},{1,2},{2,3},{3,4},{4,5},{5,6},{6,7},{7,8},{8,9},{9,10},{10,1... | collective-permute-start | bytes 2359304 | tf_op jit(solution)/shard_map/ppermute | solution.py:283
  64.9 9.2 %third_part.1 = (f32[2,512,128]{2,1,0:T(8,128)S(1)}, f32[2,2,256,256]{3,2,1,0:T(8,128)S(1)}, f32[2,2,128,256]{3,2,1,0:T(8,128)S(1)}, f32[2,2,384,128]{3,2,1,0:T(8,128)S(1)}) custom-call(s32[5,2]{1,0:T(8,128)S(1)} %broadcast_subtract_fusion.place, s32[1]{0:T(128)} %bitcast.14.count, f32[5,2,2,128,128]{4,3,2,1,0:T(8,128)} %get-tuple-element.94.windows, ...), custom_call_target="tpu_custom_call" | custom-call | flops 8053063680 | bytes 8388608 | tf_op jit(solution)/shard_map/third_part/pallas_call | solution.py:390
  75.1 3.6 %collective-permute-start.11 = (f32[2,2,384,128]{3,2,1,0:T(8,128)}, f32[2,2,384,128]{3,2,1,0:T(8,128)S(1)}, u32[]{:S(2)}, u32[]{:S(2)}) collective-permute-start(f32[2,2,384,128]{3,2,1,0:T(8,128)} %copy-done.4), channel_id=1, source_target_pairs={{0,1},{1,2},{2,3},{3,4},{4,5},{5,6},{6,7},{7,8},{8,9},{9,10},{10,1... | collective-permute-start | bytes 2359304 | tf_op jit(solution)/shard_map/ppermute | solution.py:283
  81.0 1.9 %collective-permute-start.10 = (f32[9,16,128]{2,1,0:T(8,128)S(1)}, f32[9,16,128]{2,1,0:T(8,128)S(1)}, u32[]{:S(2)}, u32[]{:S(2)}) collective-permute-start(f32[9,16,128]{2,1,0:T(8,128)S(1)} %get-tuple-element.123), channel_id=1, source_target_pairs={{0,96},{1,97},{2,98},{3,99},{4,100},{5,101},{6,102},{7,103},{8,104... | collective-permute-start | bytes 221192 | tf_op jit(solution)/shard_map/ppermute | solution.py:317
  82.8 1.5 %collective-permute-start.9 = (f32[9,16,128]{2,1,0:T(8,128)S(1)}, f32[9,16,128]{2,1,0:T(8,128)S(1)}, u32[]{:S(2)}, u32[]{:S(2)}) collective-permute-start(f32[9,16,128]{2,1,0:T(8,128)S(1)} %get-tuple-element.124), channel_id=1, source_target_pairs={{0,64},{1,65},{2,66},{3,67},{4,68},{5,69},{6,70},{7,71},{8,72},{9,... | collective-permute-start | bytes 221192 | tf_op jit(solution)/shard_map/ppermute | solution.py:317
  85.4 3.4 %collective-permute-start.18 = (f32[2,2,128,256]{3,2,1,0:T(8,128)S(1)}, f32[2,2,128,256]{3,2,1,0:T(8,128)S(1)}, u32[]{:S(2)}, u32[]{:S(2)}) collective-permute-start(f32[2,2,128,256]{3,2,1,0:T(8,128)S(1)} %add_dynamic-update-slice_fusion.3), channel_id=1, source_target_pairs={{0,32},{32,64},{64,96},{1,33},{33,65},{65,97},{2,34},{34,66},{66,9... | collective-permute-start | bytes 1572872 | tf_op jit(solution)/shard_map/ppermute | solution.py:283
  88.9 3.0 %collective-permute-start.13 = (f32[9,16,128]{2,1,0:T(8,128)S(1)}, f32[9,16,128]{2,1,0:T(8,128)S(1)}, u32[]{:S(2)}, u32[]{:S(2)}) collective-permute-start(f32[9,16,128]{2,1,0:T(8,128)S(1)} %add_add_fusion.2), channel_id=1, source_target_pairs={{0,4},{1,5},{2,6},{3,7},{4,0},{5,1},{6,2},{7,3},{8,12},{9,13},{10,... | collective-permute-start | bytes 221192 | tf_op jit(solution)/shard_map/ppermute | solution.py:323
  94.1 2.1 %collective-permute-done.14 = f32[9,16,128]{2,1,0:T(8,128)S(1)} collective-permute-done((f32[9,16,128]{2,1,0:T(8,128)S(1)}, f32[9,16,128]{2,1,0:T(8,128)S(1)}, u32[]{:S(2)}, u32[]{:S(2)}) %collective-permute-start.14) | collective-permute-done | bytes 73760 | tf_op jit(solution)/shard_map/ppermute | solution.py:323
  96.3 2.2 %collective-permute-start.16 = (f32[9,16,128]{2,1,0:T(8,128)S(1)}, f32[9,16,128]{2,1,0:T(8,128)S(1)}, u32[]{:S(2)}, u32[]{:S(2)}) collective-permute-start(f32[9,16,128]{2,1,0:T(8,128)S(1)} %add_add_fusion.1), channel_id=1, source_target_pairs={{0,16},{1,17},{2,18},{3,19},{4,20},{5,21},{6,22},{7,23},{8,24},{9,... | collective-permute-start | bytes 221192 | tf_op jit(solution)/shard_map/ppermute | solution.py:323
  98.4 2.9 %collective-permute-start.17 = (f32[9,16,128]{2,1,0:T(8,128)S(1)}, f32[9,16,128]{2,1,0:T(8,128)S(1)}, u32[]{:S(2)}, u32[]{:S(2)}) collective-permute-start(f32[9,16,128]{2,1,0:T(8,128)S(1)} %add_add_fusion.1), channel_id=1, source_target_pairs={{0,24},{1,25},{2,26},{3,27},{4,28},{5,29},{6,30},{7,31},{8,16},{9,... | collective-permute-start | bytes 221192 | tf_op jit(solution)/shard_map/ppermute | solution.py:323
  101.4 3.6 %collective-permute-start.22 = (f32[2,2,128,256]{3,2,1,0:T(8,128)S(1)}, f32[2,2,128,256]{3,2,1,0:T(8,128)S(1)}, u32[]{:S(2)}, u32[]{:S(2)}) collective-permute-start(f32[2,2,128,256]{3,2,1,0:T(8,128)S(1)} %add_dynamic-update-slice_fusion.2), channel_id=1, source_target_pairs={{0,32},{32,64},{64,96},{1,33},{33,65},{65,97},{2,34},{34,66},{66,9... | collective-permute-start | bytes 1572872 | tf_op jit(solution)/shard_map/ppermute | solution.py:283
  107.8 2.2 %collective-permute-start.21 = (f32[8,16,128]{2,1,0:T(8,128)S(1)}, f32[8,16,128]{2,1,0:T(8,128)S(1)}, u32[]{:S(2)}, u32[]{:S(2)}) collective-permute-start(f32[8,16,128]{2,1,0:T(8,128)S(1)} %get-tuple-element.115), channel_id=1, source_target_pairs={{0,96},{1,97},{2,98},{3,99},{4,100},{5,101},{6,102},{7,103},{8,104... | collective-permute-start | bytes 196616 | tf_op jit(solution)/shard_map/ppermute | solution.py:333
  110.2 6.4 %collective-permute-done.19 = f32[8,16,128]{2,1,0:T(8,128)S(1)} collective-permute-done((f32[8,16,128]{2,1,0:T(8,128)S(1)}, f32[8,16,128]{2,1,0:T(8,128)S(1)}, u32[]{:S(2)}, u32[]{:S(2)}) %collective-permute-start.19) | collective-permute-done | bytes 65568 | tf_op jit(solution)/shard_map/ppermute | solution.py:333
  118.1 2.5 %collective-permute-start.23 = (f32[8,64,128]{2,1,0:T(8,128)S(1)}, f32[8,64,128]{2,1,0:T(8,128)S(1)}, u32[]{:S(2)}, u32[]{:S(2)}) collective-permute-start(f32[8,64,128]{2,1,0:T(8,128)S(1)} %constant_dynamic-update-slice_fusion), channel_id=1, source_target_pairs={{0,1},{1,0},{2,3},{3,2},{4,5},{5,4},{6,7},{7,6},{8,9},{9,8},{10,11... | collective-permute-start | bytes 786440 | tf_op jit(solution)/shard_map/ppermute | solution.py:342
  120.7 1.6 %fusion = f32[2,4,256,256]{3,2,1,0:T(8,128)} fusion(f32[2,4,256,256]{3,2,1,0:T(8,128)S(1)} %copy-done.8, f32[2,2,256,256]{3,2,1,0:T(8,128)S(1)} %fusion.1, f32[2,2,256,256]{3,2,1,0:T(8,128)S(1)} %fusion.2), kind=kLoop, calls=%fused_computation.1 | loop fusion | flops 1572864 | bytes 6291456 | tf_op jit(solution)/shard_map/sub | solution.py:416
  (75 shorter events, 18.4 us)
Async XLA Ops:
  3.0 16.3 %collective-permute-start = (f32[2,2,128,256]{3,2,1,0:T(8,128)}, f32[2,2,128,256]{3,2,1,0:T(8,128)S(1)}, u32[]{:S(2)}, u32[]{:S(2)}) collective-permute-start(f32[2,2,128,256]{3,2,1,0:T(8,128)} %get-tuple-element.118), channel_id=1, source_target_pairs={{32,0},{64,32},{96,64},{33,1},{65,33},{97,65},{34,2},{66,34},{98,6... | collective-permute-start | bytes 1572872 | tf_op jit(solution)/shard_map/ppermute | solution.py:283
  4.5 26.1 %collective-permute-start.3 = (f32[2,2,128,256]{3,2,1,0:T(8,128)}, f32[2,2,128,256]{3,2,1,0:T(8,128)S(1)}, u32[]{:S(2)}, u32[]{:S(2)}) collective-permute-start(f32[2,2,128,256]{3,2,1,0:T(8,128)} %get-tuple-element.119), channel_id=1, source_target_pairs={{32,0},{64,32},{96,64},{33,1},{65,33},{97,65},{34,2},{66,34},{98,6... | collective-permute-start | bytes 1572872 | tf_op jit(solution)/shard_map/ppermute | solution.py:283
  6.9 26.9 %collective-permute-start.1 = (f32[2,2,256,128]{3,2,1,0:T(8,128)}, f32[2,2,256,128]{3,2,1,0:T(8,128)S(1)}, u32[]{:S(2)}, u32[]{:S(2)}) collective-permute-start(f32[2,2,256,128]{3,2,1,0:T(8,128)} %get-tuple-element.116), channel_id=1, source_target_pairs={{1,0},{2,1},{3,2},{4,3},{5,4},{6,5},{7,6},{8,7},{9,8},{10,9},{11,1... | collective-permute-start | bytes 1572872 | tf_op jit(solution)/shard_map/ppermute | solution.py:283
  10.2 33.0 %collective-permute-start.4 = (f32[2,2,256,128]{3,2,1,0:T(8,128)}, f32[2,2,256,128]{3,2,1,0:T(8,128)}, u32[]{:S(2)}, u32[]{:S(2)}) collective-permute-start(f32[2,2,256,128]{3,2,1,0:T(8,128)} %get-tuple-element.117), channel_id=1, source_target_pairs={{1,0},{2,1},{3,2},{4,3},{5,4},{6,5},{7,6},{8,7},{9,8},{10,9},{11,1... | collective-permute-start | bytes 1572872 | tf_op jit(solution)/shard_map/ppermute | solution.py:283
  20.1 13.7 %collective-permute-start.2 = (f32[2,2,128,128]{3,2,1,0:T(8,128)}, f32[2,2,128,128]{3,2,1,0:T(8,128)S(1)}, u32[]{:S(2)}, u32[]{:S(2)}) collective-permute-start(f32[2,2,128,128]{3,2,1,0:T(8,128)} %slice.234), channel_id=1, source_target_pairs={{1,0},{2,1},{3,2},{4,3},{5,4},{6,5},{7,6},{8,7},{9,8},{10,9},{11,1... | collective-permute-start | bytes 786440 | tf_op jit(solution)/shard_map/ppermute | solution.py:283
  30.6 12.6 %collective-permute-start.5 = (f32[2,2,128,128]{3,2,1,0:T(8,128)S(1)}, f32[2,2,128,128]{3,2,1,0:T(8,128)S(1)}, u32[]{:S(2)}, u32[]{:S(2)}) collective-permute-start(f32[2,2,128,128]{3,2,1,0:T(8,128)S(1)} %slice.235), channel_id=1, source_target_pairs={{1,0},{2,1},{3,2},{4,3},{5,4},{6,5},{7,6},{8,7},{9,8},{10,9},{11,1... | collective-permute-start | bytes 786440 | tf_op jit(solution)/shard_map/ppermute | solution.py:283
  62.0 13.0 %collective-permute-start.6 = (f32[2,2,384,128]{3,2,1,0:T(8,128)}, f32[2,2,384,128]{3,2,1,0:T(8,128)}, u32[]{:S(2)}, u32[]{:S(2)}) collective-permute-start(f32[2,2,384,128]{3,2,1,0:T(8,128)} %get-tuple-element.100), channel_id=1, source_target_pairs={{0,1},{1,2},{2,3},{3,4},{4,5},{5,6},{6,7},{7,8},{8,9},{9,10},{10,1... | collective-permute-start | bytes 2359304 | tf_op jit(solution)/shard_map/ppermute | solution.py:283
  75.0 4.9 %collective-permute-start.7 = (f32[9,64,128]{2,1,0:T(8,128)S(1)}, f32[9,64,128]{2,1,0:T(8,128)}, u32[]{:S(2)}, u32[]{:S(2)}) collective-permute-start(f32[9,64,128]{2,1,0:T(8,128)S(1)} %fusion.3), channel_id=1, source_target_pairs={{0,1},{1,0},{2,3},{3,2},{4,5},{5,4},{6,7},{7,6},{8,9},{9,8},{10,11... | collective-permute-start | bytes 884744 | tf_op jit(solution)/shard_map/ppermute | solution.py:316
  75.1 13.7 %collective-permute-start.11 = (f32[2,2,384,128]{3,2,1,0:T(8,128)}, f32[2,2,384,128]{3,2,1,0:T(8,128)S(1)}, u32[]{:S(2)}, u32[]{:S(2)}) collective-permute-start(f32[2,2,384,128]{3,2,1,0:T(8,128)} %copy-done.4), channel_id=1, source_target_pairs={{0,1},{1,2},{2,3},{3,4},{4,5},{5,6},{6,7},{7,8},{8,9},{9,10},{10,1... | collective-permute-start | bytes 2359304 | tf_op jit(solution)/shard_map/ppermute | solution.py:283
  81.0 7.8 %collective-permute-start.10 = (f32[9,16,128]{2,1,0:T(8,128)S(1)}, f32[9,16,128]{2,1,0:T(8,128)S(1)}, u32[]{:S(2)}, u32[]{:S(2)}) collective-permute-start(f32[9,16,128]{2,1,0:T(8,128)S(1)} %get-tuple-element.123), channel_id=1, source_target_pairs={{0,96},{1,97},{2,98},{3,99},{4,100},{5,101},{6,102},{7,103},{8,104... | collective-permute-start | bytes 221192 | tf_op jit(solution)/shard_map/ppermute | solution.py:317
  82.8 6.0 %collective-permute-start.9 = (f32[9,16,128]{2,1,0:T(8,128)S(1)}, f32[9,16,128]{2,1,0:T(8,128)S(1)}, u32[]{:S(2)}, u32[]{:S(2)}) collective-permute-start(f32[9,16,128]{2,1,0:T(8,128)S(1)} %get-tuple-element.124), channel_id=1, source_target_pairs={{0,64},{1,65},{2,66},{3,67},{4,68},{5,69},{6,70},{7,71},{8,72},{9,... | collective-permute-start | bytes 221192 | tf_op jit(solution)/shard_map/ppermute | solution.py:317
  84.4 4.5 %collective-permute-start.8 = (f32[9,16,128]{2,1,0:T(8,128)S(1)}, f32[9,16,128]{2,1,0:T(8,128)S(1)}, u32[]{:S(2)}, u32[]{:S(2)}) collective-permute-start(f32[9,16,128]{2,1,0:T(8,128)S(1)} %get-tuple-element.122), channel_id=1, source_target_pairs={{0,32},{1,33},{2,34},{3,35},{4,36},{5,37},{6,38},{7,39},{8,40},{9,... | collective-permute-start | bytes 221192 | tf_op jit(solution)/shard_map/ppermute | solution.py:317
  85.4 19.7 %collective-permute-start.18 = (f32[2,2,128,256]{3,2,1,0:T(8,128)S(1)}, f32[2,2,128,256]{3,2,1,0:T(8,128)S(1)}, u32[]{:S(2)}, u32[]{:S(2)}) collective-permute-start(f32[2,2,128,256]{3,2,1,0:T(8,128)S(1)} %add_dynamic-update-slice_fusion.3), channel_id=1, source_target_pairs={{0,32},{32,64},{64,96},{1,33},{33,65},{65,97},{2,34},{34,66},{66,9... | collective-permute-start | bytes 1572872 | tf_op jit(solution)/shard_map/ppermute | solution.py:283
  88.9 5.2 %collective-permute-start.13 = (f32[9,16,128]{2,1,0:T(8,128)S(1)}, f32[9,16,128]{2,1,0:T(8,128)S(1)}, u32[]{:S(2)}, u32[]{:S(2)}) collective-permute-start(f32[9,16,128]{2,1,0:T(8,128)S(1)} %add_add_fusion.2), channel_id=1, source_target_pairs={{0,4},{1,5},{2,6},{3,7},{4,0},{5,1},{6,2},{7,3},{8,12},{9,13},{10,... | collective-permute-start | bytes 221192 | tf_op jit(solution)/shard_map/ppermute | solution.py:323
  91.8 4.4 %collective-permute-start.14 = (f32[9,16,128]{2,1,0:T(8,128)S(1)}, f32[9,16,128]{2,1,0:T(8,128)S(1)}, u32[]{:S(2)}, u32[]{:S(2)}) collective-permute-start(f32[9,16,128]{2,1,0:T(8,128)S(1)} %add_add_fusion.2), channel_id=1, source_target_pairs={{0,6},{1,7},{2,4},{3,5},{4,2},{5,3},{6,0},{7,1},{8,14},{9,15},{10,... | collective-permute-start | bytes 221192 | tf_op jit(solution)/shard_map/ppermute | solution.py:323
  92.9 3.3 %collective-permute-start.12 = (f32[9,16,128]{2,1,0:T(8,128)S(1)}, f32[9,16,128]{2,1,0:T(8,128)S(1)}, u32[]{:S(2)}, u32[]{:S(2)}) collective-permute-start(f32[9,16,128]{2,1,0:T(8,128)S(1)} %add_add_fusion.2), channel_id=1, source_target_pairs={{0,2},{1,3},{2,0},{3,1},{4,6},{5,7},{6,4},{7,5},{8,10},{9,11},{10,... | collective-permute-start | bytes 221192 | tf_op jit(solution)/shard_map/ppermute | solution.py:323
  96.3 8.7 %collective-permute-start.16 = (f32[9,16,128]{2,1,0:T(8,128)S(1)}, f32[9,16,128]{2,1,0:T(8,128)S(1)}, u32[]{:S(2)}, u32[]{:S(2)}) collective-permute-start(f32[9,16,128]{2,1,0:T(8,128)S(1)} %add_add_fusion.1), channel_id=1, source_target_pairs={{0,16},{1,17},{2,18},{3,19},{4,20},{5,21},{6,22},{7,23},{8,24},{9,... | collective-permute-start | bytes 221192 | tf_op jit(solution)/shard_map/ppermute | solution.py:323
  98.4 6.6 %collective-permute-start.17 = (f32[9,16,128]{2,1,0:T(8,128)S(1)}, f32[9,16,128]{2,1,0:T(8,128)S(1)}, u32[]{:S(2)}, u32[]{:S(2)}) collective-permute-start(f32[9,16,128]{2,1,0:T(8,128)S(1)} %add_add_fusion.1), channel_id=1, source_target_pairs={{0,24},{1,25},{2,26},{3,27},{4,28},{5,29},{6,30},{7,31},{8,16},{9,... | collective-permute-start | bytes 221192 | tf_op jit(solution)/shard_map/ppermute | solution.py:323
  101.4 3.7 %collective-permute-start.15 = (f32[9,16,128]{2,1,0:T(8,128)S(1)}, f32[9,16,128]{2,1,0:T(8,128)S(1)}, u32[]{:S(2)}, u32[]{:S(2)}) collective-permute-start(f32[9,16,128]{2,1,0:T(8,128)S(1)} %add_add_fusion.1), channel_id=1, source_target_pairs={{0,8},{1,9},{2,10},{3,11},{4,12},{5,13},{6,14},{7,15},{8,0},{9,1},... | collective-permute-start | bytes 221192 | tf_op jit(solution)/shard_map/ppermute | solution.py:323
  101.4 16.6 %collective-permute-start.22 = (f32[2,2,128,256]{3,2,1,0:T(8,128)S(1)}, f32[2,2,128,256]{3,2,1,0:T(8,128)S(1)}, u32[]{:S(2)}, u32[]{:S(2)}) collective-permute-start(f32[2,2,128,256]{3,2,1,0:T(8,128)S(1)} %add_dynamic-update-slice_fusion.2), channel_id=1, source_target_pairs={{0,32},{32,64},{64,96},{1,33},{33,65},{65,97},{2,34},{34,66},{66,9... | collective-permute-start | bytes 1572872 | tf_op jit(solution)/shard_map/ppermute | solution.py:283
  106.1 10.5 %collective-permute-start.19 = (f32[8,16,128]{2,1,0:T(8,128)S(1)}, f32[8,16,128]{2,1,0:T(8,128)S(1)}, u32[]{:S(2)}, u32[]{:S(2)}) collective-permute-start(f32[8,16,128]{2,1,0:T(8,128)S(1)} %get-tuple-element.115), channel_id=1, source_target_pairs={{0,32},{1,33},{2,34},{3,35},{4,36},{5,37},{6,38},{7,39},{8,40},{9,... | collective-permute-start | bytes 196616 | tf_op jit(solution)/shard_map/ppermute | solution.py:333
  107.4 10.6 %collective-permute-start.20 = (f32[8,16,128]{2,1,0:T(8,128)S(1)}, f32[8,16,128]{2,1,0:T(8,128)S(1)}, u32[]{:S(2)}, u32[]{:S(2)}) collective-permute-start(f32[8,16,128]{2,1,0:T(8,128)S(1)} %get-tuple-element.115), channel_id=1, source_target_pairs={{0,64},{1,65},{2,66},{3,67},{4,68},{5,69},{6,70},{7,71},{8,72},{9,... | collective-permute-start | bytes 196616 | tf_op jit(solution)/shard_map/ppermute | solution.py:333
  107.8 10.2 %collective-permute-start.21 = (f32[8,16,128]{2,1,0:T(8,128)S(1)}, f32[8,16,128]{2,1,0:T(8,128)S(1)}, u32[]{:S(2)}, u32[]{:S(2)}) collective-permute-start(f32[8,16,128]{2,1,0:T(8,128)S(1)} %get-tuple-element.115), channel_id=1, source_target_pairs={{0,96},{1,97},{2,98},{3,99},{4,100},{5,101},{6,102},{7,103},{8,104... | collective-permute-start | bytes 196616 | tf_op jit(solution)/shard_map/ppermute | solution.py:333
  118.1 4.2 %collective-permute-start.23 = (f32[8,64,128]{2,1,0:T(8,128)S(1)}, f32[8,64,128]{2,1,0:T(8,128)S(1)}, u32[]{:S(2)}, u32[]{:S(2)}) collective-permute-start(f32[8,64,128]{2,1,0:T(8,128)S(1)} %constant_dynamic-update-slice_fusion), channel_id=1, source_target_pairs={{0,1},{1,0},{2,3},{3,2},{4,5},{5,4},{6,7},{7,6},{8,9},{9,8},{10,11... | collective-permute-start | bytes 786440 | tf_op jit(solution)/shard_map/ppermute | solution.py:342
  (10 other events, 127.2 us)

commit v3 on v2

--- a/solution.py
+++ b/solution.py
@@ -283,6 +283,12 @@
     return lax.ppermute(value, axis, [(source, source + steps) for source in range(leading, last)])
 
 
+def diagonal(value):
+    rows, cols = lax.axis_size("row"), lax.axis_size("col")
+    pairs = [(a * cols + b, (a - 1) * cols + b - 1) for a in range(1, rows) for b in range(1, cols)]
+    return lax.ppermute(value, AXES, pairs)
+
+
 def mesh_perm(move):
     pairs = []
     for z in range(4):
@@ -354,12 +360,13 @@
     count = counts[0]
     waves = probe.reshape(WAVE)
 
-    bottoms, rights, corners = [], [], []
+    bottoms, rights = [], []
     for first in (0, 2):
         piece = object_field[:, first : first + 2]
         bottoms.append(shifted(piece[:, :, :N, :], "row", -1))
         rights.append(shifted(piece[:, :, :, :N], "col", -1))
-        corners.append(shifted(bottoms[-1][:, :, :, :N], "col", -1))
+
+    corners = [shifted(bottoms[0][:, :, :, :N], "col", -1), diagonal(object_field[:, 2:, :N, :N])]
 
     windows, wave1, wave2, weight = pl.pallas_call(
         first_half,
@@ -373,6 +380,7 @@
         name="first_half",
     )(place, count, object_field, bottoms[0], rights[0], corners[0], waves, tables)
 
+    wave2, bottoms[1] = lax.optimization_barrier((wave2, bottoms[1]))
     grad_specs = [HBM, HBM, HBM]
     grad_shapes = [f32(2, 2, TILE, TILE), f32(2, 2, N, TILE), f32(2, 2, EXT, N)]
     grad2, *late = pl.pallas_call(

time: 125 us -> 125 us (level)
  Pallas kernels: 36.4 us -> 23.1 us
  starting transfers between devices: 46.8 us -> 59.8 us
  local copies, waits for them, and re-layouts: 7.11 us -> 9.1 us
    pallas_call x1, Pallas kernels: 17.9 us -> 10.4 us  [shards(): pl.pallas_call(second_half, grid=(slots,), in_specs=[SMEM, SMEM, HBM, HBM...]
    ppermute x3, starting transfers between devices: 3.39 us -> 10.2 us  [share_of_sum(): lax.ppermute(part(total, z ^ k, QUARTER), AXES, ALONG_Z[k])]
    unnamed x20 -> x24, local copies, waits for them, and re-layouts: 2.74 us -> 5.78 us
    pallas_call x1, Pallas kernels: 9.35 us -> 6.33 us  [shards(): pl.pallas_call(first_half, grid=(slots,), in_specs=[SMEM, SMEM, HBM, HBM,...]
    pallas_call x1, Pallas kernels: 9.15 us -> 6.31 us  [shards(): pl.pallas_call(third_part, grid=(slots,), in_specs=[SMEM, SMEM, per_slot(...]
    ppermute x10 -> x9, starting transfers between devices: 27.7 us -> 30.4 us  [shifted(): lax.ppermute(value, axis, [(source, source + steps) for source in range(l...]
    ppermute x1, starting transfers between devices: 2.5 us -> 5.23 us  [gather_whole(): other = lax.ppermute(half, AXES, SWAP_CORE)]
    ppermute x10 -> x9, waiting for transfers between devices: 12.9 us -> 11 us  [shifted(): lax.ppermute(value, axis, [(source, source + steps) for source in range(l...]
  transfers between devices with their start and end apart: 24 -> 24, of which waited for: 6 -> 9; matrix products, arithmetic and copies ran while one was open for 7% -> 6% of each run, Pallas kernels for 15% -> 10%
where the time goes in v3:
time: 125 us; the launch traced here: 124 us
  starting transfers between devices  59.8 us (48%)
  Pallas kernels  23.1 us (18%)
  waiting for transfers between devices  23 us (18%)
  local copies, waits for them, and re-layouts  9.1 us (7%)
  other arithmetic  7.21 us (6%)
  between operations  1.75 us (1%)
    ppermute x9, starting transfers between devices, shifted(): lax.ppermute(value, axis, [(source, source + steps) for source in range(l...  30.4 us
    ppermute x9, waiting for transfers between devices, shifted(): lax.ppermute(value, axis, [(source, source + steps) for source in range(l...  11 us
    pallas_call x1, Pallas kernels, shards(): pl.pallas_call(second_half, grid=(slots,), in_specs=[SMEM, SMEM, HBM, HBM...  10.4 us
    ppermute x3, starting transfers between devices, share_of_sum(): lax.ppermute(part(total, z ^ k, QUARTER), AXES, ALONG_Z[k])  10.2 us
    ppermute x6, starting transfers between devices, sum_plane(): arrived = [total] + [lax.ppermute(total, AXES, along[k]) for k in (1, 2, 3)]  8.59 us
    ppermute x3, waiting for transfers between devices, gather_half(): arrived = [mine] + [lax.ppermute(mine, AXES, ALONG_Z[k]) for k in (1, 2, 3)]  6.4 us
    pallas_call x1, Pallas kernels, shards(): pl.pallas_call(first_half, grid=(slots,), in_specs=[SMEM, SMEM, HBM, HBM,...  6.33 us
    pallas_call x1, Pallas kernels, shards(): pl.pallas_call(third_part, grid=(slots,), in_specs=[SMEM, SMEM, per_slot(...  6.31 us
  transfers between devices with their start and end apart: 24, of which 9 were waited for; matrix products, arithmetic and copies ran while one was open for 6% of the time, Pallas kernels for 10%

profile of v3, /device:TPU:1, one launch (start us, length us, event | category | flops | bytes accessed | tf_op | source)
XLA Modules:
  0.0 123.9 jit_solution(7313291341440433239)
XLA Ops:
  0.6 2.2 %fusion.7 = (f32[2,2,128,256]{3,2,1,0:T(8,128)}, f32[2,2,128,256]{3,2,1,0:T(8,128)S(1)}) fusion(f32[2,4,256,256]{3,2,1,0:T(8,128)} %own.3), kind=kLoop, calls=%fused_computation.35 | loop fusion | bytes 2097152 | tf_op jit(solution)/shard_map/slice | solution.py:366
  2.9 1.4 %collective-permute-start = (f32[2,2,128,256]{3,2,1,0:T(8,128)S(1)}, f32[2,2,128,256]{3,2,1,0:T(8,128)S(1)}, u32[]{:S(2)}, u32[]{:S(2)}) collective-permute-start(f32[2,2,128,256]{3,2,1,0:T(8,128)S(1)} %get-tuple-element.123), channel_id=1, source_target_pairs={{32,0},{64,32},{96,64},{33,1},{65,33},{97,65},{34,2},{66,34},{98,6... | collective-permute-start | bytes 1572872 | tf_op jit(solution)/shard_map/ppermute | solution.py:283
  5.2 3.3 %collective-permute-start.1 = (f32[2,2,256,128]{3,2,1,0:T(8,128)S(1)}, f32[2,2,256,128]{3,2,1,0:T(8,128)S(1)}, u32[]{:S(2)}, u32[]{:S(2)}) collective-permute-start(f32[2,2,256,128]{3,2,1,0:T(8,128)S(1)} %get-tuple-element.121), channel_id=1, source_target_pairs={{1,0},{2,1},{3,2},{4,3},{5,4},{6,5},{7,6},{8,7},{9,8},{10,9},{11,1... | collective-permute-start | bytes 1572872 | tf_op jit(solution)/shard_map/ppermute | solution.py:283
  9.8 1.9 %collective-permute-start.4 = (f32[2,2,256,128]{3,2,1,0:T(8,128)}, f32[2,2,256,128]{3,2,1,0:T(8,128)}, u32[]{:S(2)}, u32[]{:S(2)}) collective-permute-start(f32[2,2,256,128]{3,2,1,0:T(8,128)} %get-tuple-element.120), channel_id=1, source_target_pairs={{1,0},{2,1},{3,2},{4,3},{5,4},{6,5},{7,6},{8,7},{9,8},{10,9},{11,1... | collective-permute-start | bytes 1572872 | tf_op jit(solution)/shard_map/ppermute | solution.py:283
  13.1 5.9 %collective-permute-done.bottom = f32[2,2,128,256]{3,2,1,0:T(8,128)S(1)} collective-permute-done((f32[2,2,128,256]{3,2,1,0:T(8,128)S(1)}, f32[2,2,128,256]{3,2,1,0:T(8,128)S(1)}, u32[]{:S(2)}, u32[]{:S(2)}) %collective-permute-start) | collective-permute-done | bytes 524320 | tf_op jit(solution)/shard_map/ppermute | solution.py:283
  19.0 4.0 %collective-permute-start.2 = (f32[2,2,128,128]{3,2,1,0:T(8,128)S(1)}, f32[2,2,128,128]{3,2,1,0:T(8,128)S(1)}, u32[]{:S(2)}, u32[]{:S(2)}) collective-permute-start(f32[2,2,128,128]{3,2,1,0:T(8,128)S(1)} %slice.234), channel_id=1, source_target_pairs={{1,0},{2,1},{3,2},{4,3},{5,4},{6,5},{7,6},{8,7},{9,8},{10,9},{11,1... | collective-permute-start | bytes 786440 | tf_op jit(solution)/shard_map/ppermute | solution.py:283
  24.7 4.1 %collective-permute-done.2.corner = f32[2,2,128,128]{3,2,1,0:T(8,128)S(1)} collective-permute-done((f32[2,2,128,128]{3,2,1,0:T(8,128)S(1)}, f32[2,2,128,128]{3,2,1,0:T(8,128)S(1)}, u32[]{:S(2)}, u32[]{:S(2)}) %collective-permute-start.2) | collective-permute-done | bytes 262176 | tf_op jit(solution)/shard_map/ppermute | solution.py:283
  31.0 6.3 %first_half.1 = (f32[5,2,2,128,128]{4,3,2,1,0:T(8,128)}, f32[5,2,512,128]{3,2,1,0:T(8,128)}, f32[5,2,512,128]{3,2,1,0:T(8,128)}, f32[128,128]{1,0:T(8,128)S(1)}) custom-call(s32[5,2]{1,0:T(8,128)S(1)} %broadcast_subtract_fusion.place, s32[1]{0:T(128)} %bitcast.12.count, f32[2,4,256,256]{3,2,1,0:T(8,128)} %own.3, ...), custom_call_target="tpu_custom_call" | custom-call | flops 8053063680 | bytes 8388608 | tf_op jit(solution)/shard_map/first_half/pallas_call | solution.py:371
  37.4 10.4 %second_half.1 = (f32[5,2,512,128]{3,2,1,0:T(8,128)}, f32[2,2,256,256]{3,2,1,0:T(8,128)S(1)}, f32[2,2,128,256]{3,2,1,0:T(8,128)S(1)}, f32[2,2,384,128]{3,2,1,0:T(8,128)}) custom-call(s32[5,2]{1,0:T(8,128)S(1)} %broadcast_subtract_fusion.place, s32[1]{0:T(128)} %bitcast.13.count, f32[2,4,256,256]{3,2,1,0:T(8,128)} %own.3, ...), custom_call_target="tpu_custom_call" | custom-call | flops 16106127360 | bytes 8388608 | tf_op jit(solution)/shard_map/second_half/pallas_call | solution.py:386
  48.6 2.8 %collective-permute-start.6 = (f32[2,2,384,128]{3,2,1,0:T(8,128)}, f32[2,2,384,128]{3,2,1,0:T(8,128)}, u32[]{:S(2)}, u32[]{:S(2)}) collective-permute-start(f32[2,2,384,128]{3,2,1,0:T(8,128)} %get-tuple-element.104), channel_id=1, source_target_pairs={{0,1},{1,2},{2,3},{3,4},{4,5},{5,6},{6,7},{7,8},{8,9},{9,10},{10,1... | collective-permute-start | bytes 2359304 | tf_op jit(solution)/shard_map/ppermute | solution.py:283
  52.5 6.3 %third_part.1 = (f32[2,512,128]{2,1,0:T(8,128)S(1)}, f32[2,2,256,256]{3,2,1,0:T(8,128)S(1)}, f32[2,2,128,256]{3,2,1,0:T(8,128)S(1)}, f32[2,2,384,128]{3,2,1,0:T(8,128)S(1)}) custom-call(s32[5,2]{1,0:T(8,128)S(1)} %broadcast_subtract_fusion.place, s32[1]{0:T(128)} %bitcast.14.count, f32[5,2,2,128,128]{4,3,2,1,0:T(8,128)} %get-tuple-element.96.windows, ...), custom_call_target="tpu_custom_call" | custom-call | flops 8053063680 | bytes 8388608 | tf_op jit(solution)/shard_map/third_part/pallas_call | solution.py:398
  60.8 9.8 %collective-permute-start.11 = (f32[2,2,384,128]{3,2,1,0:T(8,128)}, f32[2,2,384,128]{3,2,1,0:T(8,128)S(1)}, u32[]{:S(2)}, u32[]{:S(2)}) collective-permute-start(f32[2,2,384,128]{3,2,1,0:T(8,128)} %copy-done.4), channel_id=1, source_target_pairs={{0,1},{1,2},{2,3},{3,4},{4,5},{5,6},{6,7},{7,8},{8,9},{9,10},{10,1... | collective-permute-start | bytes 2359304 | tf_op jit(solution)/shard_map/ppermute | solution.py:283
  72.8 9.5 %collective-permute-start.10 = (f32[9,16,128]{2,1,0:T(8,128)S(1)}, f32[9,16,128]{2,1,0:T(8,128)S(1)}, u32[]{:S(2)}, u32[]{:S(2)}) collective-permute-start(f32[9,16,128]{2,1,0:T(8,128)S(1)} %get-tuple-element.127), channel_id=1, source_target_pairs={{0,96},{1,97},{2,98},{3,99},{4,100},{5,101},{6,102},{7,103},{8,104... | collective-permute-start | bytes 221192 | tf_op jit(solution)/shard_map/ppermute | solution.py:323
  84.1 2.7 %collective-permute-start.18 = (f32[2,2,128,256]{3,2,1,0:T(8,128)S(1)}, f32[2,2,128,256]{3,2,1,0:T(8,128)S(1)}, u32[]{:S(2)}, u32[]{:S(2)}) collective-permute-start(f32[2,2,128,256]{3,2,1,0:T(8,128)S(1)} %add_dynamic-update-slice_fusion.3), channel_id=1, source_target_pairs={{0,32},{32,64},{64,96},{1,33},{33,65},{65,97},{2,34},{34,66},{66,9... | collective-permute-start | bytes 1572872 | tf_op jit(solution)/shard_map/ppermute | solution.py:283
  88.0 2.3 %collective-permute-start.13 = (f32[9,16,128]{2,1,0:T(8,128)S(1)}, f32[9,16,128]{2,1,0:T(8,128)S(1)}, u32[]{:S(2)}, u32[]{:S(2)}) collective-permute-start(f32[9,16,128]{2,1,0:T(8,128)S(1)} %add_add_fusion.2), channel_id=1, source_target_pairs={{0,4},{1,5},{2,6},{3,7},{4,0},{5,1},{6,2},{7,3},{8,12},{9,13},{10,... | collective-permute-start | bytes 221192 | tf_op jit(solution)/shard_map/ppermute | solution.py:329
  90.3 2.3 %collective-permute-start.14 = (f32[9,16,128]{2,1,0:T(8,128)S(1)}, f32[9,16,128]{2,1,0:T(8,128)S(1)}, u32[]{:S(2)}, u32[]{:S(2)}) collective-permute-start(f32[9,16,128]{2,1,0:T(8,128)S(1)} %add_add_fusion.2), channel_id=1, source_target_pairs={{0,6},{1,7},{2,4},{3,5},{4,2},{5,3},{6,0},{7,1},{8,14},{9,15},{10,... | collective-permute-start | bytes 221192 | tf_op jit(solution)/shard_map/ppermute | solution.py:329
  93.2 2.3 %collective-permute-done.14 = f32[9,16,128]{2,1,0:T(8,128)S(1)} collective-permute-done((f32[9,16,128]{2,1,0:T(8,128)S(1)}, f32[9,16,128]{2,1,0:T(8,128)S(1)}, u32[]{:S(2)}, u32[]{:S(2)}) %collective-permute-start.14) | collective-permute-done | bytes 73760 | tf_op jit(solution)/shard_map/ppermute | solution.py:329
  96.5 3.5 %collective-permute-start.16 = (f32[9,16,128]{2,1,0:T(8,128)S(1)}, f32[9,16,128]{2,1,0:T(8,128)S(1)}, u32[]{:S(2)}, u32[]{:S(2)}) collective-permute-start(f32[9,16,128]{2,1,0:T(8,128)S(1)} %add_add_fusion.1), channel_id=1, source_target_pairs={{0,16},{1,17},{2,18},{3,19},{4,20},{5,21},{6,22},{7,23},{8,24},{9,... | collective-permute-start | bytes 221192 | tf_op jit(solution)/shard_map/ppermute | solution.py:329
  100.1 3.2 %collective-permute-start.22 = (f32[2,2,128,256]{3,2,1,0:T(8,128)S(1)}, f32[2,2,128,256]{3,2,1,0:T(8,128)S(1)}, u32[]{:S(2)}, u32[]{:S(2)}) collective-permute-start(f32[2,2,128,256]{3,2,1,0:T(8,128)S(1)} %add_dynamic-update-slice_fusion.2), channel_id=1, source_target_pairs={{0,32},{32,64},{64,96},{1,33},{33,65},{65,97},{2,34},{34,66},{66,9... | collective-permute-start | bytes 1572872 | tf_op jit(solution)/shard_map/ppermute | solution.py:283
  106.9 2.3 %collective-permute-start.20 = (f32[8,16,128]{2,1,0:T(8,128)S(1)}, f32[8,16,128]{2,1,0:T(8,128)S(1)}, u32[]{:S(2)}, u32[]{:S(2)}) collective-permute-start(f32[8,16,128]{2,1,0:T(8,128)S(1)} %get-tuple-element.119), channel_id=1, source_target_pairs={{0,64},{1,65},{2,66},{3,67},{4,68},{5,69},{6,70},{7,71},{8,72},{9,... | collective-permute-start | bytes 196616 | tf_op jit(solution)/shard_map/ppermute | solution.py:339
  109.6 3.5 %collective-permute-done.19 = f32[8,16,128]{2,1,0:T(8,128)S(1)} collective-permute-done((f32[8,16,128]{2,1,0:T(8,128)S(1)}, f32[8,16,128]{2,1,0:T(8,128)S(1)}, u32[]{:S(2)}, u32[]{:S(2)}) %collective-permute-start.19) | collective-permute-done | bytes 65568 | tf_op jit(solution)/shard_map/ppermute | solution.py:339
  113.1 2.9 %collective-permute-done.20 = f32[8,16,128]{2,1,0:T(8,128)S(1)} collective-permute-done((f32[8,16,128]{2,1,0:T(8,128)S(1)}, f32[8,16,128]{2,1,0:T(8,128)S(1)}, u32[]{:S(2)}, u32[]{:S(2)}) %collective-permute-start.20) | collective-permute-done | bytes 65568 | tf_op jit(solution)/shard_map/ppermute | solution.py:339
  116.1 5.2 %collective-permute-start.23 = (f32[8,64,128]{2,1,0:T(8,128)S(1)}, f32[8,64,128]{2,1,0:T(8,128)S(1)}, u32[]{:S(2)}, u32[]{:S(2)}) collective-permute-start(f32[8,64,128]{2,1,0:T(8,128)S(1)} %constant_dynamic-update-slice_fusion), channel_id=1, source_target_pairs={{0,1},{1,0},{2,3},{3,2},{4,5},{5,4},{6,7},{7,6},{8,9},{9,8},{10,11... | collective-permute-start | bytes 786440 | tf_op jit(solution)/shard_map/ppermute | solution.py:348
  121.4 1.6 %fusion = f32[2,4,256,256]{3,2,1,0:T(8,128)} fusion(f32[2,4,256,256]{3,2,1,0:T(8,128)S(1)} %copy-done.10, f32[2,2,256,256]{3,2,1,0:T(8,128)S(1)} %fusion.1, f32[2,2,256,256]{3,2,1,0:T(8,128)S(1)} %fusion.2), kind=kLoop, calls=%fused_computation.1 | loop fusion | flops 1572864 | bytes 6291456 | tf_op jit(solution)/shard_map/sub | solution.py:424
  (79 shorter events, 22.3 us)
Async XLA Ops:
  2.9 16.1 %collective-permute-start = (f32[2,2,128,256]{3,2,1,0:T(8,128)S(1)}, f32[2,2,128,256]{3,2,1,0:T(8,128)S(1)}, u32[]{:S(2)}, u32[]{:S(2)}) collective-permute-start(f32[2,2,128,256]{3,2,1,0:T(8,128)S(1)} %get-tuple-element.123), channel_id=1, source_target_pairs={{32,0},{64,32},{96,64},{33,1},{65,33},{97,65},{34,2},{66,34},{98,6... | collective-permute-start | bytes 1572872 | tf_op jit(solution)/shard_map/ppermute | solution.py:283
  5.2 18.7 %collective-permute-start.1 = (f32[2,2,256,128]{3,2,1,0:T(8,128)S(1)}, f32[2,2,256,128]{3,2,1,0:T(8,128)S(1)}, u32[]{:S(2)}, u32[]{:S(2)}) collective-permute-start(f32[2,2,256,128]{3,2,1,0:T(8,128)S(1)} %get-tuple-element.121), channel_id=1, source_target_pairs={{1,0},{2,1},{3,2},{4,3},{5,4},{6,5},{7,6},{8,7},{9,8},{10,9},{11,1... | collective-permute-start | bytes 1572872 | tf_op jit(solution)/shard_map/ppermute | solution.py:283
  8.5 28.8 %collective-permute-start.3 = (f32[2,2,128,256]{3,2,1,0:T(8,128)}, f32[2,2,128,256]{3,2,1,0:T(8,128)}, u32[]{:S(2)}, u32[]{:S(2)}) collective-permute-start(f32[2,2,128,256]{3,2,1,0:T(8,128)} %get-tuple-element.122), channel_id=1, source_target_pairs={{32,0},{64,32},{96,64},{33,1},{65,33},{97,65},{34,2},{66,34},{98,6... | collective-permute-start | bytes 1572872 | tf_op jit(solution)/shard_map/ppermute | solution.py:283
  9.8 27.5 %collective-permute-start.4 = (f32[2,2,256,128]{3,2,1,0:T(8,128)}, f32[2,2,256,128]{3,2,1,0:T(8,128)}, u32[]{:S(2)}, u32[]{:S(2)}) collective-permute-start(f32[2,2,256,128]{3,2,1,0:T(8,128)} %get-tuple-element.120), channel_id=1, source_target_pairs={{1,0},{2,1},{3,2},{4,3},{5,4},{6,5},{7,6},{8,7},{9,8},{10,9},{11,1... | collective-permute-start | bytes 1572872 | tf_op jit(solution)/shard_map/ppermute | solution.py:283
  11.8 25.6 %collective-permute-start.5 = (f32[2,2,128,128]{3,2,1,0:T(8,128)S(1)}, f32[2,2,128,128]{3,2,1,0:T(8,128)S(1)}, u32[]{:S(2)}, u32[]{:S(2)}) collective-permute-start(f32[2,2,128,128]{3,2,1,0:T(8,128)S(1)} %slice.221), channel_id=1, source_target_pairs={{33,0},{34,1},{35,2},{36,3},{37,4},{38,5},{39,6},{40,7},{41,8},{42... | collective-permute-start | bytes 786440 | tf_op jit(solution)/shard_map/ppermute | solution.py:289
  19.0 9.7 %collective-permute-start.2 = (f32[2,2,128,128]{3,2,1,0:T(8,128)S(1)}, f32[2,2,128,128]{3,2,1,0:T(8,128)S(1)}, u32[]{:S(2)}, u32[]{:S(2)}) collective-permute-start(f32[2,2,128,128]{3,2,1,0:T(8,128)S(1)} %slice.234), channel_id=1, source_target_pairs={{1,0},{2,1},{3,2},{4,3},{5,4},{6,5},{7,6},{8,7},{9,8},{10,9},{11,1... | collective-permute-start | bytes 786440 | tf_op jit(solution)/shard_map/ppermute | solution.py:283
  48.6 12.0 %collective-permute-start.6 = (f32[2,2,384,128]{3,2,1,0:T(8,128)}, f32[2,2,384,128]{3,2,1,0:T(8,128)}, u32[]{:S(2)}, u32[]{:S(2)}) collective-permute-start(f32[2,2,384,128]{3,2,1,0:T(8,128)} %get-tuple-element.104), channel_id=1, source_target_pairs={{0,1},{1,2},{2,3},{3,4},{4,5},{5,6},{6,7},{7,8},{8,9},{9,10},{10,1... | collective-permute-start | bytes 2359304 | tf_op jit(solution)/shard_map/ppermute | solution.py:283
  60.7 11.1 %collective-permute-start.7 = (f32[9,64,128]{2,1,0:T(8,128)S(1)}, f32[9,64,128]{2,1,0:T(8,128)}, u32[]{:S(2)}, u32[]{:S(2)}) collective-permute-start(f32[9,64,128]{2,1,0:T(8,128)S(1)} %fusion.3), channel_id=1, source_target_pairs={{0,1},{1,0},{2,3},{3,2},{4,5},{5,4},{6,7},{7,6},{8,9},{9,8},{10,11... | collective-permute-start | bytes 884744 | tf_op jit(solution)/shard_map/ppermute | solution.py:322
  60.8 27.1 %collective-permute-start.11 = (f32[2,2,384,128]{3,2,1,0:T(8,128)}, f32[2,2,384,128]{3,2,1,0:T(8,128)S(1)}, u32[]{:S(2)}, u32[]{:S(2)}) collective-permute-start(f32[2,2,384,128]{3,2,1,0:T(8,128)} %copy-done.4), channel_id=1, source_target_pairs={{0,1},{1,2},{2,3},{3,4},{4,5},{5,6},{6,7},{7,8},{8,9},{9,10},{10,1... | collective-permute-start | bytes 2359304 | tf_op jit(solution)/shard_map/ppermute | solution.py:283
  72.8 14.0 %collective-permute-start.10 = (f32[9,16,128]{2,1,0:T(8,128)S(1)}, f32[9,16,128]{2,1,0:T(8,128)S(1)}, u32[]{:S(2)}, u32[]{:S(2)}) collective-permute-start(f32[9,16,128]{2,1,0:T(8,128)S(1)} %get-tuple-element.127), channel_id=1, source_target_pairs={{0,96},{1,97},{2,98},{3,99},{4,100},{5,101},{6,102},{7,103},{8,104... | collective-permute-start | bytes 221192 | tf_op jit(solution)/shard_map/ppermute | solution.py:323
  82.4 5.6 %collective-permute-start.9 = (f32[9,16,128]{2,1,0:T(8,128)S(1)}, f32[9,16,128]{2,1,0:T(8,128)S(1)}, u32[]{:S(2)}, u32[]{:S(2)}) collective-permute-start(f32[9,16,128]{2,1,0:T(8,128)S(1)} %get-tuple-element.128), channel_id=1, source_target_pairs={{0,64},{1,65},{2,66},{3,67},{4,68},{5,69},{6,70},{7,71},{8,72},{9,... | collective-permute-start | bytes 221192 | tf_op jit(solution)/shard_map/ppermute | solution.py:323
  82.4 5.6 %collective-permute-start.8 = (f32[9,16,128]{2,1,0:T(8,128)S(1)}, f32[9,16,128]{2,1,0:T(8,128)S(1)}, u32[]{:S(2)}, u32[]{:S(2)}) collective-permute-start(f32[9,16,128]{2,1,0:T(8,128)S(1)} %get-tuple-element.126), channel_id=1, source_target_pairs={{0,32},{1,33},{2,34},{3,35},{4,36},{5,37},{6,38},{7,39},{8,40},{9,... | collective-permute-start | bytes 221192 | tf_op jit(solution)/shard_map/ppermute | solution.py:323
  84.1 20.4 %collective-permute-start.18 = (f32[2,2,128,256]{3,2,1,0:T(8,128)S(1)}, f32[2,2,128,256]{3,2,1,0:T(8,128)S(1)}, u32[]{:S(2)}, u32[]{:S(2)}) collective-permute-start(f32[2,2,128,256]{3,2,1,0:T(8,128)S(1)} %add_dynamic-update-slice_fusion.3), channel_id=1, source_target_pairs={{0,32},{32,64},{64,96},{1,33},{33,65},{65,97},{2,34},{34,66},{66,9... | collective-permute-start | bytes 1572872 | tf_op jit(solution)/shard_map/ppermute | solution.py:283
  88.0 5.2 %collective-permute-start.13 = (f32[9,16,128]{2,1,0:T(8,128)S(1)}, f32[9,16,128]{2,1,0:T(8,128)S(1)}, u32[]{:S(2)}, u32[]{:S(2)}) collective-permute-start(f32[9,16,128]{2,1,0:T(8,128)S(1)} %add_add_fusion.2), channel_id=1, source_target_pairs={{0,4},{1,5},{2,6},{3,7},{4,0},{5,1},{6,2},{7,3},{8,12},{9,13},{10,... | collective-permute-start | bytes 221192 | tf_op jit(solution)/shard_map/ppermute | solution.py:329
  90.3 5.2 %collective-permute-start.14 = (f32[9,16,128]{2,1,0:T(8,128)S(1)}, f32[9,16,128]{2,1,0:T(8,128)S(1)}, u32[]{:S(2)}, u32[]{:S(2)}) collective-permute-start(f32[9,16,128]{2,1,0:T(8,128)S(1)} %add_add_fusion.2), channel_id=1, source_target_pairs={{0,6},{1,7},{2,4},{3,5},{4,2},{5,3},{6,0},{7,1},{8,14},{9,15},{10,... | collective-permute-start | bytes 221192 | tf_op jit(solution)/shard_map/ppermute | solution.py:329
  92.6 3.9 %collective-permute-start.12 = (f32[9,16,128]{2,1,0:T(8,128)S(1)}, f32[9,16,128]{2,1,0:T(8,128)S(1)}, u32[]{:S(2)}, u32[]{:S(2)}) collective-permute-start(f32[9,16,128]{2,1,0:T(8,128)S(1)} %add_add_fusion.2), channel_id=1, source_target_pairs={{0,2},{1,3},{2,0},{3,1},{4,6},{5,7},{6,4},{7,5},{8,10},{9,11},{10,... | collective-permute-start | bytes 221192 | tf_op jit(solution)/shard_map/ppermute | solution.py:329
  96.5 6.7 %collective-permute-start.16 = (f32[9,16,128]{2,1,0:T(8,128)S(1)}, f32[9,16,128]{2,1,0:T(8,128)S(1)}, u32[]{:S(2)}, u32[]{:S(2)}) collective-permute-start(f32[9,16,128]{2,1,0:T(8,128)S(1)} %add_add_fusion.1), channel_id=1, source_target_pairs={{0,16},{1,17},{2,18},{3,19},{4,20},{5,21},{6,22},{7,23},{8,24},{9,... | collective-permute-start | bytes 221192 | tf_op jit(solution)/shard_map/ppermute | solution.py:329
  100.0 4.4 %collective-permute-start.17 = (f32[9,16,128]{2,1,0:T(8,128)S(1)}, f32[9,16,128]{2,1,0:T(8,128)S(1)}, u32[]{:S(2)}, u32[]{:S(2)}) collective-permute-start(f32[9,16,128]{2,1,0:T(8,128)S(1)} %add_add_fusion.1), channel_id=1, source_target_pairs={{0,24},{1,25},{2,26},{3,27},{4,28},{5,29},{6,30},{7,31},{8,16},{9,... | collective-permute-start | bytes 221192 | tf_op jit(solution)/shard_map/ppermute | solution.py:329
  100.0 4.4 %collective-permute-start.15 = (f32[9,16,128]{2,1,0:T(8,128)S(1)}, f32[9,16,128]{2,1,0:T(8,128)S(1)}, u32[]{:S(2)}, u32[]{:S(2)}) collective-permute-start(f32[9,16,128]{2,1,0:T(8,128)S(1)} %add_add_fusion.1), channel_id=1, source_target_pairs={{0,8},{1,9},{2,10},{3,11},{4,12},{5,13},{6,14},{7,15},{8,0},{9,1},... | collective-permute-start | bytes 221192 | tf_op jit(solution)/shard_map/ppermute | solution.py:329
  100.1 16.0 %collective-permute-start.22 = (f32[2,2,128,256]{3,2,1,0:T(8,128)S(1)}, f32[2,2,128,256]{3,2,1,0:T(8,128)S(1)}, u32[]{:S(2)}, u32[]{:S(2)}) collective-permute-start(f32[2,2,128,256]{3,2,1,0:T(8,128)S(1)} %add_dynamic-update-slice_fusion.2), channel_id=1, source_target_pairs={{0,32},{32,64},{64,96},{1,33},{33,65},{65,97},{2,34},{34,66},{66,9... | collective-permute-start | bytes 1572872 | tf_op jit(solution)/shard_map/ppermute | solution.py:283
  105.5 7.6 %collective-permute-start.19 = (f32[8,16,128]{2,1,0:T(8,128)S(1)}, f32[8,16,128]{2,1,0:T(8,128)S(1)}, u32[]{:S(2)}, u32[]{:S(2)}) collective-permute-start(f32[8,16,128]{2,1,0:T(8,128)S(1)} %get-tuple-element.119), channel_id=1, source_target_pairs={{0,32},{1,33},{2,34},{3,35},{4,36},{5,37},{6,38},{7,39},{8,40},{9,... | collective-permute-start | bytes 196616 | tf_op jit(solution)/shard_map/ppermute | solution.py:339
  106.9 9.2 %collective-permute-start.20 = (f32[8,16,128]{2,1,0:T(8,128)S(1)}, f32[8,16,128]{2,1,0:T(8,128)S(1)}, u32[]{:S(2)}, u32[]{:S(2)}) collective-permute-start(f32[8,16,128]{2,1,0:T(8,128)S(1)} %get-tuple-element.119), channel_id=1, source_target_pairs={{0,64},{1,65},{2,66},{3,67},{4,68},{5,69},{6,70},{7,71},{8,72},{9,... | collective-permute-start | bytes 196616 | tf_op jit(solution)/shard_map/ppermute | solution.py:339
  109.1 6.9 %collective-permute-start.21 = (f32[8,16,128]{2,1,0:T(8,128)S(1)}, f32[8,16,128]{2,1,0:T(8,128)S(1)}, u32[]{:S(2)}, u32[]{:S(2)}) collective-permute-start(f32[8,16,128]{2,1,0:T(8,128)S(1)} %get-tuple-element.119), channel_id=1, source_target_pairs={{0,96},{1,97},{2,98},{3,99},{4,100},{5,101},{6,102},{7,103},{8,104... | collective-permute-start | bytes 196616 | tf_op jit(solution)/shard_map/ppermute | solution.py:339
  116.1 7.0 %collective-permute-start.23 = (f32[8,64,128]{2,1,0:T(8,128)S(1)}, f32[8,64,128]{2,1,0:T(8,128)S(1)}, u32[]{:S(2)}, u32[]{:S(2)}) collective-permute-start(f32[8,64,128]{2,1,0:T(8,128)S(1)} %constant_dynamic-update-slice_fusion), channel_id=1, source_target_pairs={{0,1},{1,0},{2,3},{3,2},{4,5},{5,4},{6,7},{7,6},{8,9},{9,8},{10,11... | collective-permute-start | bytes 786440 | tf_op jit(solution)/shard_map/ppermute | solution.py:348
  (12 other events, 101.1 us)

commit v4 on v3

--- a/solution.py
+++ b/solution.py
@@ -137,15 +137,17 @@
         ext[part, depth, tile + k, pl.ds(row, N), :] += block[:, k * N : (k + 1) * N]
 
 
-def run_copies(pairs, sems):
+def run_copies(pairs, sems, zeroed=None):
     copies = [pltpu.make_async_copy(*pair, sems.at[k]) for k, pair in enumerate(pairs)]
     for copy in copies:
         copy.start()
+    if zeroed is not None:
+        zeroed[...] = jnp.zeros_like(zeroed)
     for copy in copies:
         copy.wait()
 
 
-def load_extended(first, own, bottom, right, corner, ext, sems):
+def load_extended(first, own, bottom, right, corner, ext, sems, zeroed=None):
     upper, lower = pl.ds(0, TILE), pl.ds(TILE, N)
     pairs = []
     for k in range(2):
@@ -154,7 +156,7 @@
         pairs.append((bottom.at[:, :, :, lanes], ext.at[:, :, k, lower]))
     pairs.append((right, ext.at[:, :, 2, upper]))
     pairs.append((corner, ext.at[:, :, 2, lower]))
-    run_copies(pairs, sems)
+    run_copies(pairs, sems, zeroed)
 
 
 def store_gradient(ext, own, bottom, right, sems):
@@ -181,8 +183,7 @@
 
     @pl.when(slot == 0)
     def _():
-        load_extended(0, own, bottom, right, corner, ext, sems)
-        weight[...] = jnp.zeros_like(weight)
+        load_extended(0, own, bottom, right, corner, ext, sems, weight)
 
     @pl.when(slot < count[0])
     def _():
@@ -204,8 +205,7 @@
 
     @pl.when(slot == 0)
     def _():
-        load_extended(2, own, bottom, right, corner, ext, sems)
-        grad[...] = jnp.zeros_like(grad)
+        load_extended(2, own, bottom, right, corner, ext, sems, grad)
 
     @pl.when(slot < count[0])
     def _():

time: 125 us -> 125 us (level)
  Pallas kernels: 23.1 us -> 36.4 us
  starting transfers between devices: 59.8 us -> 47.6 us
  waiting for transfers between devices: 23 us -> 21.6 us
    ppermute x9, starting transfers between devices: 30.4 us -> 22.1 us  [shifted(): lax.ppermute(value, axis, [(source, source + steps) for source in range(l...]
    pallas_call x1, Pallas kernels: 10.4 us -> 17.9 us  [shards(): pl.pallas_call(second_half, grid=(slots,), in_specs=[SMEM, SMEM, HBM, HBM...]
    ppermute x3, starting transfers between devices: 10.2 us -> 4.42 us  [share_of_sum(): lax.ppermute(part(total, z ^ k, QUARTER), AXES, ALONG_Z[k])]
    pallas_call x1, Pallas kernels: 6.33 us -> 9.33 us  [shards(): pl.pallas_call(first_half, grid=(slots,), in_specs=[SMEM, SMEM, HBM, HBM,...]
    pallas_call x1, Pallas kernels: 6.31 us -> 9.16 us  [shards(): pl.pallas_call(third_part, grid=(slots,), in_specs=[SMEM, SMEM, per_slot(...]
    ppermute x1, starting transfers between devices: 0.09 us -> 1.42 us  [share_of_sum(): lax.ppermute(part(total, 1 - core, rows), AXES, SWAP_CORE)]
  transfers between devices with their start and end apart: 24 -> 24, of which waited for: 9 -> 8; matrix products, arithmetic and copies ran while one was open for 6% -> 6% of each run, Pallas kernels for 10% -> 15%
where the time goes in v4:
time: 125 us; the launch traced here: 124 us
  starting transfers between devices  47.6 us (38%)
  Pallas kernels  36.4 us (29%)
  waiting for transfers between devices  21.6 us (17%)
  local copies, waits for them, and re-layouts  9.1 us (7%)
  other arithmetic  7.22 us (6%)
  between operations  1.7 us (1%)
    ppermute x9, starting transfers between devices, shifted(): lax.ppermute(value, axis, [(source, source + steps) for source in range(l...  22.1 us
    pallas_call x1, Pallas kernels, shards(): pl.pallas_call(second_half, grid=(slots,), in_specs=[SMEM, SMEM, HBM, HBM...  17.9 us
    ppermute x9, waiting for transfers between devices, shifted(): lax.ppermute(value, axis, [(source, source + steps) for source in range(l...  10 us
    ppermute x6, starting transfers between devices, sum_plane(): arrived = [total] + [lax.ppermute(total, AXES, along[k]) for k in (1, 2, 3)]  9.83 us
    pallas_call x1, Pallas kernels, shards(): pl.pallas_call(first_half, grid=(slots,), in_specs=[SMEM, SMEM, HBM, HBM,...  9.33 us
    pallas_call x1, Pallas kernels, shards(): pl.pallas_call(third_part, grid=(slots,), in_specs=[SMEM, SMEM, per_slot(...  9.16 us
    ppermute x3, waiting for transfers between devices, gather_half(): arrived = [mine] + [lax.ppermute(mine, AXES, ALONG_Z[k]) for k in (1, 2, 3)]  6.48 us
    unnamed x24, local copies, waits for them, and re-layouts  5.78 us
  transfers between devices with their start and end apart: 24, of which 8 were waited for; matrix products, arithmetic and copies ran while one was open for 6% of the time, Pallas kernels for 15%

profile of v4, /device:TPU:1, one launch (start us, length us, event | category | flops | bytes accessed | tf_op | source)
XLA Modules:
  0.0 123.6 jit_solution(8674497566025169560)
XLA Ops:
  0.6 2.2 %fusion.7 = (f32[2,2,128,256]{3,2,1,0:T(8,128)}, f32[2,2,128,256]{3,2,1,0:T(8,128)S(1)}) fusion(f32[2,4,256,256]{3,2,1,0:T(8,128)} %own.3), kind=kLoop, calls=%fused_computation.35 | loop fusion | bytes 2097152 | tf_op jit(solution)/shard_map/slice | solution.py:366
  5.2 3.3 %collective-permute-start.1 = (f32[2,2,256,128]{3,2,1,0:T(8,128)S(1)}, f32[2,2,256,128]{3,2,1,0:T(8,128)S(1)}, u32[]{:S(2)}, u32[]{:S(2)}) collective-permute-start(f32[2,2,256,128]{3,2,1,0:T(8,128)S(1)} %get-tuple-element.121), channel_id=1, source_target_pairs={{1,0},{2,1},{3,2},{4,3},{5,4},{6,5},{7,6},{8,7},{9,8},{10,9},{11,1... | collective-permute-start | bytes 1572872 | tf_op jit(solution)/shard_map/ppermute | solution.py:283
  9.8 1.9 %collective-permute-start.4 = (f32[2,2,256,128]{3,2,1,0:T(8,128)}, f32[2,2,256,128]{3,2,1,0:T(8,128)}, u32[]{:S(2)}, u32[]{:S(2)}) collective-permute-start(f32[2,2,256,128]{3,2,1,0:T(8,128)} %get-tuple-element.120), channel_id=1, source_target_pairs={{1,0},{2,1},{3,2},{4,3},{5,4},{6,5},{7,6},{8,7},{9,8},{10,9},{11,1... | collective-permute-start | bytes 1572872 | tf_op jit(solution)/shard_map/ppermute | solution.py:283
  13.1 5.9 %collective-permute-done.bottom = f32[2,2,128,256]{3,2,1,0:T(8,128)S(1)} collective-permute-done((f32[2,2,128,256]{3,2,1,0:T(8,128)S(1)}, f32[2,2,128,256]{3,2,1,0:T(8,128)S(1)}, u32[]{:S(2)}, u32[]{:S(2)}) %collective-permute-start) | collective-permute-done | bytes 524320 | tf_op jit(solution)/shard_map/ppermute | solution.py:283
  19.0 4.0 %collective-permute-start.2 = (f32[2,2,128,128]{3,2,1,0:T(8,128)S(1)}, f32[2,2,128,128]{3,2,1,0:T(8,128)S(1)}, u32[]{:S(2)}, u32[]{:S(2)}) collective-permute-start(f32[2,2,128,128]{3,2,1,0:T(8,128)S(1)} %slice.234), channel_id=1, source_target_pairs={{1,0},{2,1},{3,2},{4,3},{5,4},{6,5},{7,6},{8,7},{9,8},{10,9},{11,1... | collective-permute-start | bytes 786440 | tf_op jit(solution)/shard_map/ppermute | solution.py:283
  24.7 4.1 %collective-permute-done.2.corner = f32[2,2,128,128]{3,2,1,0:T(8,128)S(1)} collective-permute-done((f32[2,2,128,128]{3,2,1,0:T(8,128)S(1)}, f32[2,2,128,128]{3,2,1,0:T(8,128)S(1)}, u32[]{:S(2)}, u32[]{:S(2)}) %collective-permute-start.2) | collective-permute-done | bytes 262176 | tf_op jit(solution)/shard_map/ppermute | solution.py:283
  31.0 9.3 %first_half.1 = (f32[5,2,2,128,128]{4,3,2,1,0:T(8,128)}, f32[5,2,512,128]{3,2,1,0:T(8,128)}, f32[5,2,512,128]{3,2,1,0:T(8,128)}, f32[128,128]{1,0:T(8,128)S(1)}) custom-call(s32[5,2]{1,0:T(8,128)S(1)} %broadcast_subtract_fusion.place, s32[1]{0:T(128)} %bitcast.12.count, f32[2,4,256,256]{3,2,1,0:T(8,128)} %own.3, ...), custom_call_target="tpu_custom_call" | custom-call | flops 8053063680 | bytes 8388608 | tf_op jit(solution)/shard_map/first_half/pallas_call | solution.py:371
  40.4 17.9 %second_half.1 = (f32[5,2,512,128]{3,2,1,0:T(8,128)}, f32[2,2,256,256]{3,2,1,0:T(8,128)S(1)}, f32[2,2,128,256]{3,2,1,0:T(8,128)S(1)}, f32[2,2,384,128]{3,2,1,0:T(8,128)}) custom-call(s32[5,2]{1,0:T(8,128)S(1)} %broadcast_subtract_fusion.place, s32[1]{0:T(128)} %bitcast.13.count, f32[2,4,256,256]{3,2,1,0:T(8,128)} %own.3, ...), custom_call_target="tpu_custom_call" | custom-call | flops 16106127360 | bytes 8388608 | tf_op jit(solution)/shard_map/second_half/pallas_call | solution.py:386
  59.1 1.9 %collective-permute-start.6 = (f32[2,2,384,128]{3,2,1,0:T(8,128)}, f32[2,2,384,128]{3,2,1,0:T(8,128)}, u32[]{:S(2)}, u32[]{:S(2)}) collective-permute-start(f32[2,2,384,128]{3,2,1,0:T(8,128)} %get-tuple-element.104), channel_id=1, source_target_pairs={{0,1},{1,2},{2,3},{3,4},{4,5},{5,6},{6,7},{7,8},{8,9},{9,10},{10,1... | collective-permute-start | bytes 2359304 | tf_op jit(solution)/shard_map/ppermute | solution.py:283
  62.1 9.2 %third_part.1 = (f32[2,512,128]{2,1,0:T(8,128)S(1)}, f32[2,2,256,256]{3,2,1,0:T(8,128)S(1)}, f32[2,2,128,256]{3,2,1,0:T(8,128)S(1)}, f32[2,2,384,128]{3,2,1,0:T(8,128)S(1)}) custom-call(s32[5,2]{1,0:T(8,128)S(1)} %broadcast_subtract_fusion.place, s32[1]{0:T(128)} %bitcast.14.count, f32[5,2,2,128,128]{4,3,2,1,0:T(8,128)} %get-tuple-element.96.windows, ...), custom_call_target="tpu_custom_call" | custom-call | flops 8053063680 | bytes 8388608 | tf_op jit(solution)/shard_map/third_part/pallas_call | solution.py:398
  72.1 1.4 %collective-permute-start.7 = (f32[9,64,128]{2,1,0:T(8,128)S(1)}, f32[9,64,128]{2,1,0:T(8,128)}, u32[]{:S(2)}, u32[]{:S(2)}) collective-permute-start(f32[9,64,128]{2,1,0:T(8,128)S(1)} %fusion.3), channel_id=1, source_target_pairs={{0,1},{1,0},{2,3},{3,2},{4,5},{5,4},{6,7},{7,6},{8,9},{9,8},{10,11... | collective-permute-start | bytes 884744 | tf_op jit(solution)/shard_map/ppermute | solution.py:322
  73.6 2.0 %collective-permute-start.11 = (f32[2,2,384,128]{3,2,1,0:T(8,128)}, f32[2,2,384,128]{3,2,1,0:T(8,128)S(1)}, u32[]{:S(2)}, u32[]{:S(2)}) collective-permute-start(f32[2,2,384,128]{3,2,1,0:T(8,128)} %copy-done.4), channel_id=1, source_target_pairs={{0,1},{1,2},{2,3},{3,4},{4,5},{5,6},{6,7},{7,8},{8,9},{9,10},{10,1... | collective-permute-start | bytes 2359304 | tf_op jit(solution)/shard_map/ppermute | solution.py:283
  77.8 3.3 %collective-permute-start.10 = (f32[9,16,128]{2,1,0:T(8,128)S(1)}, f32[9,16,128]{2,1,0:T(8,128)S(1)}, u32[]{:S(2)}, u32[]{:S(2)}) collective-permute-start(f32[9,16,128]{2,1,0:T(8,128)S(1)} %get-tuple-element.127), channel_id=1, source_target_pairs={{0,96},{1,97},{2,98},{3,99},{4,100},{5,101},{6,102},{7,103},{8,104... | collective-permute-start | bytes 221192 | tf_op jit(solution)/shard_map/ppermute | solution.py:323
  83.2 3.4 %collective-permute-start.18 = (f32[2,2,128,256]{3,2,1,0:T(8,128)S(1)}, f32[2,2,128,256]{3,2,1,0:T(8,128)S(1)}, u32[]{:S(2)}, u32[]{:S(2)}) collective-permute-start(f32[2,2,128,256]{3,2,1,0:T(8,128)S(1)} %add_dynamic-update-slice_fusion.3), channel_id=1, source_target_pairs={{0,32},{32,64},{64,96},{1,33},{33,65},{65,97},{2,34},{34,66},{66,9... | collective-permute-start | bytes 1572872 | tf_op jit(solution)/shard_map/ppermute | solution.py:283
  86.7 4.6 %collective-permute-start.13 = (f32[9,16,128]{2,1,0:T(8,128)S(1)}, f32[9,16,128]{2,1,0:T(8,128)S(1)}, u32[]{:S(2)}, u32[]{:S(2)}) collective-permute-start(f32[9,16,128]{2,1,0:T(8,128)S(1)} %add_add_fusion.2), channel_id=1, source_target_pairs={{0,4},{1,5},{2,6},{3,7},{4,0},{5,1},{6,2},{7,3},{8,12},{9,13},{10,... | collective-permute-start | bytes 221192 | tf_op jit(solution)/shard_map/ppermute | solution.py:329
  91.4 1.8 %collective-permute-start.14 = (f32[9,16,128]{2,1,0:T(8,128)S(1)}, f32[9,16,128]{2,1,0:T(8,128)S(1)}, u32[]{:S(2)}, u32[]{:S(2)}) collective-permute-start(f32[9,16,128]{2,1,0:T(8,128)S(1)} %add_add_fusion.2), channel_id=1, source_target_pairs={{0,6},{1,7},{2,4},{3,5},{4,2},{5,3},{6,0},{7,1},{8,14},{9,15},{10,... | collective-permute-start | bytes 221192 | tf_op jit(solution)/shard_map/ppermute | solution.py:329
  93.9 2.5 %collective-permute-done.14 = f32[9,16,128]{2,1,0:T(8,128)S(1)} collective-permute-done((f32[9,16,128]{2,1,0:T(8,128)S(1)}, f32[9,16,128]{2,1,0:T(8,128)S(1)}, u32[]{:S(2)}, u32[]{:S(2)}) %collective-permute-start.14) | collective-permute-done | bytes 73760 | tf_op jit(solution)/shard_map/ppermute | solution.py:329
  97.4 2.9 %collective-permute-start.16 = (f32[9,16,128]{2,1,0:T(8,128)S(1)}, f32[9,16,128]{2,1,0:T(8,128)S(1)}, u32[]{:S(2)}, u32[]{:S(2)}) collective-permute-start(f32[9,16,128]{2,1,0:T(8,128)S(1)} %add_add_fusion.1), channel_id=1, source_target_pairs={{0,16},{1,17},{2,18},{3,19},{4,20},{5,21},{6,22},{7,23},{8,24},{9,... | collective-permute-start | bytes 221192 | tf_op jit(solution)/shard_map/ppermute | solution.py:329
  100.4 2.8 %collective-permute-start.22 = (f32[2,2,128,256]{3,2,1,0:T(8,128)S(1)}, f32[2,2,128,256]{3,2,1,0:T(8,128)S(1)}, u32[]{:S(2)}, u32[]{:S(2)}) collective-permute-start(f32[2,2,128,256]{3,2,1,0:T(8,128)S(1)} %add_dynamic-update-slice_fusion.2), channel_id=1, source_target_pairs={{0,32},{32,64},{64,96},{1,33},{33,65},{65,97},{2,34},{34,66},{66,9... | collective-permute-start | bytes 1572872 | tf_op jit(solution)/shard_map/ppermute | solution.py:283
  103.2 1.5 %collective-permute-done.17 = f32[9,16,128]{2,1,0:T(8,128)S(1)} collective-permute-done((f32[9,16,128]{2,1,0:T(8,128)S(1)}, f32[9,16,128]{2,1,0:T(8,128)S(1)}, u32[]{:S(2)}, u32[]{:S(2)}) %collective-permute-start.17) | collective-permute-done | bytes 73760 | tf_op jit(solution)/shard_map/ppermute | solution.py:329
  106.7 2.1 %collective-permute-start.20 = (f32[8,16,128]{2,1,0:T(8,128)S(1)}, f32[8,16,128]{2,1,0:T(8,128)S(1)}, u32[]{:S(2)}, u32[]{:S(2)}) collective-permute-start(f32[8,16,128]{2,1,0:T(8,128)S(1)} %get-tuple-element.119), channel_id=1, source_target_pairs={{0,64},{1,65},{2,66},{3,67},{4,68},{5,69},{6,70},{7,71},{8,72},{9,... | collective-permute-start | bytes 196616 | tf_op jit(solution)/shard_map/ppermute | solution.py:339
  109.9 5.1 %collective-permute-done.19 = f32[8,16,128]{2,1,0:T(8,128)S(1)} collective-permute-done((f32[8,16,128]{2,1,0:T(8,128)S(1)}, f32[8,16,128]{2,1,0:T(8,128)S(1)}, u32[]{:S(2)}, u32[]{:S(2)}) %collective-permute-start.19) | collective-permute-done | bytes 65568 | tf_op jit(solution)/shard_map/ppermute | solution.py:339
  116.4 4.6 %collective-permute-start.23 = (f32[8,64,128]{2,1,0:T(8,128)S(1)}, f32[8,64,128]{2,1,0:T(8,128)S(1)}, u32[]{:S(2)}, u32[]{:S(2)}) collective-permute-start(f32[8,64,128]{2,1,0:T(8,128)S(1)} %constant_dynamic-update-slice_fusion), channel_id=1, source_target_pairs={{0,1},{1,0},{2,3},{3,2},{4,5},{5,4},{6,7},{7,6},{8,9},{9,8},{10,11... | collective-permute-start | bytes 786440 | tf_op jit(solution)/shard_map/ppermute | solution.py:348
  121.1 1.6 %fusion = f32[2,4,256,256]{3,2,1,0:T(8,128)} fusion(f32[2,4,256,256]{3,2,1,0:T(8,128)S(1)} %copy-done.10, f32[2,2,256,256]{3,2,1,0:T(8,128)S(1)} %fusion.1, f32[2,2,256,256]{3,2,1,0:T(8,128)S(1)} %fusion.2), kind=kLoop, calls=%fused_computation.1 | loop fusion | flops 1572864 | bytes 6291456 | tf_op jit(solution)/shard_map/sub | solution.py:424
  (79 shorter events, 22.5 us)
Async XLA Ops:
  2.9 16.1 %collective-permute-start = (f32[2,2,128,256]{3,2,1,0:T(8,128)S(1)}, f32[2,2,128,256]{3,2,1,0:T(8,128)S(1)}, u32[]{:S(2)}, u32[]{:S(2)}) collective-permute-start(f32[2,2,128,256]{3,2,1,0:T(8,128)S(1)} %get-tuple-element.123), channel_id=1, source_target_pairs={{32,0},{64,32},{96,64},{33,1},{65,33},{97,65},{34,2},{66,34},{98,6... | collective-permute-start | bytes 1572872 | tf_op jit(solution)/shard_map/ppermute | solution.py:283
  5.2 18.7 %collective-permute-start.1 = (f32[2,2,256,128]{3,2,1,0:T(8,128)S(1)}, f32[2,2,256,128]{3,2,1,0:T(8,128)S(1)}, u32[]{:S(2)}, u32[]{:S(2)}) collective-permute-start(f32[2,2,256,128]{3,2,1,0:T(8,128)S(1)} %get-tuple-element.121), channel_id=1, source_target_pairs={{1,0},{2,1},{3,2},{4,3},{5,4},{6,5},{7,6},{8,7},{9,8},{10,9},{11,1... | collective-permute-start | bytes 1572872 | tf_op jit(solution)/shard_map/ppermute | solution.py:283
  8.5 31.8 %collective-permute-start.3 = (f32[2,2,128,256]{3,2,1,0:T(8,128)}, f32[2,2,128,256]{3,2,1,0:T(8,128)}, u32[]{:S(2)}, u32[]{:S(2)}) collective-permute-start(f32[2,2,128,256]{3,2,1,0:T(8,128)} %get-tuple-element.122), channel_id=1, source_target_pairs={{32,0},{64,32},{96,64},{33,1},{65,33},{97,65},{34,2},{66,34},{98,6... | collective-permute-start | bytes 1572872 | tf_op jit(solution)/shard_map/ppermute | solution.py:283
  9.8 30.6 %collective-permute-start.4 = (f32[2,2,256,128]{3,2,1,0:T(8,128)}, f32[2,2,256,128]{3,2,1,0:T(8,128)}, u32[]{:S(2)}, u32[]{:S(2)}) collective-permute-start(f32[2,2,256,128]{3,2,1,0:T(8,128)} %get-tuple-element.120), channel_id=1, source_target_pairs={{1,0},{2,1},{3,2},{4,3},{5,4},{6,5},{7,6},{8,7},{9,8},{10,9},{11,1... | collective-permute-start | bytes 1572872 | tf_op jit(solution)/shard_map/ppermute | solution.py:283
  11.8 28.6 %collective-permute-start.5 = (f32[2,2,128,128]{3,2,1,0:T(8,128)S(1)}, f32[2,2,128,128]{3,2,1,0:T(8,128)S(1)}, u32[]{:S(2)}, u32[]{:S(2)}) collective-permute-start(f32[2,2,128,128]{3,2,1,0:T(8,128)S(1)} %slice.221), channel_id=1, source_target_pairs={{33,0},{34,1},{35,2},{36,3},{37,4},{38,5},{39,6},{40,7},{41,8},{42... | collective-permute-start | bytes 786440 | tf_op jit(solution)/shard_map/ppermute | solution.py:289
  19.0 9.7 %collective-permute-start.2 = (f32[2,2,128,128]{3,2,1,0:T(8,128)S(1)}, f32[2,2,128,128]{3,2,1,0:T(8,128)S(1)}, u32[]{:S(2)}, u32[]{:S(2)}) collective-permute-start(f32[2,2,128,128]{3,2,1,0:T(8,128)S(1)} %slice.234), channel_id=1, source_target_pairs={{1,0},{2,1},{3,2},{4,3},{5,4},{6,5},{7,6},{8,7},{9,8},{10,9},{11,1... | collective-permute-start | bytes 786440 | tf_op jit(solution)/shard_map/ppermute | solution.py:283
  59.1 13.0 %collective-permute-start.6 = (f32[2,2,384,128]{3,2,1,0:T(8,128)}, f32[2,2,384,128]{3,2,1,0:T(8,128)}, u32[]{:S(2)}, u32[]{:S(2)}) collective-permute-start(f32[2,2,384,128]{3,2,1,0:T(8,128)} %get-tuple-element.104), channel_id=1, source_target_pairs={{0,1},{1,2},{2,3},{3,4},{4,5},{5,6},{6,7},{7,8},{8,9},{9,10},{10,1... | collective-permute-start | bytes 2359304 | tf_op jit(solution)/shard_map/ppermute | solution.py:283
  72.1 4.6 %collective-permute-start.7 = (f32[9,64,128]{2,1,0:T(8,128)S(1)}, f32[9,64,128]{2,1,0:T(8,128)}, u32[]{:S(2)}, u32[]{:S(2)}) collective-permute-start(f32[9,64,128]{2,1,0:T(8,128)S(1)} %fusion.3), channel_id=1, source_target_pairs={{0,1},{1,0},{2,3},{3,2},{4,5},{5,4},{6,7},{7,6},{8,9},{9,8},{10,11... | collective-permute-start | bytes 884744 | tf_op jit(solution)/shard_map/ppermute | solution.py:322
  73.6 13.2 %collective-permute-start.11 = (f32[2,2,384,128]{3,2,1,0:T(8,128)}, f32[2,2,384,128]{3,2,1,0:T(8,128)S(1)}, u32[]{:S(2)}, u32[]{:S(2)}) collective-permute-start(f32[2,2,384,128]{3,2,1,0:T(8,128)} %copy-done.4), channel_id=1, source_target_pairs={{0,1},{1,2},{2,3},{3,4},{4,5},{5,6},{6,7},{7,8},{8,9},{9,10},{10,1... | collective-permute-start | bytes 2359304 | tf_op jit(solution)/shard_map/ppermute | solution.py:283
  77.8 8.8 %collective-permute-start.10 = (f32[9,16,128]{2,1,0:T(8,128)S(1)}, f32[9,16,128]{2,1,0:T(8,128)S(1)}, u32[]{:S(2)}, u32[]{:S(2)}) collective-permute-start(f32[9,16,128]{2,1,0:T(8,128)S(1)} %get-tuple-element.127), channel_id=1, source_target_pairs={{0,96},{1,97},{2,98},{3,99},{4,100},{5,101},{6,102},{7,103},{8,104... | collective-permute-start | bytes 221192 | tf_op jit(solution)/shard_map/ppermute | solution.py:323
  81.1 5.5 %collective-permute-start.9 = (f32[9,16,128]{2,1,0:T(8,128)S(1)}, f32[9,16,128]{2,1,0:T(8,128)S(1)}, u32[]{:S(2)}, u32[]{:S(2)}) collective-permute-start(f32[9,16,128]{2,1,0:T(8,128)S(1)} %get-tuple-element.128), channel_id=1, source_target_pairs={{0,64},{1,65},{2,66},{3,67},{4,68},{5,69},{6,70},{7,71},{8,72},{9,... | collective-permute-start | bytes 221192 | tf_op jit(solution)/shard_map/ppermute | solution.py:323
  82.2 4.5 %collective-permute-start.8 = (f32[9,16,128]{2,1,0:T(8,128)S(1)}, f32[9,16,128]{2,1,0:T(8,128)S(1)}, u32[]{:S(2)}, u32[]{:S(2)}) collective-permute-start(f32[9,16,128]{2,1,0:T(8,128)S(1)} %get-tuple-element.126), channel_id=1, source_target_pairs={{0,32},{1,33},{2,34},{3,35},{4,36},{5,37},{6,38},{7,39},{8,40},{9,... | collective-permute-start | bytes 221192 | tf_op jit(solution)/shard_map/ppermute | solution.py:323
  83.2 21.5 %collective-permute-start.18 = (f32[2,2,128,256]{3,2,1,0:T(8,128)S(1)}, f32[2,2,128,256]{3,2,1,0:T(8,128)S(1)}, u32[]{:S(2)}, u32[]{:S(2)}) collective-permute-start(f32[2,2,128,256]{3,2,1,0:T(8,128)S(1)} %add_dynamic-update-slice_fusion.3), channel_id=1, source_target_pairs={{0,32},{32,64},{64,96},{1,33},{33,65},{65,97},{2,34},{34,66},{66,9... | collective-permute-start | bytes 1572872 | tf_op jit(solution)/shard_map/ppermute | solution.py:283
  86.7 7.2 %collective-permute-start.13 = (f32[9,16,128]{2,1,0:T(8,128)S(1)}, f32[9,16,128]{2,1,0:T(8,128)S(1)}, u32[]{:S(2)}, u32[]{:S(2)}) collective-permute-start(f32[9,16,128]{2,1,0:T(8,128)S(1)} %add_add_fusion.2), channel_id=1, source_target_pairs={{0,4},{1,5},{2,6},{3,7},{4,0},{5,1},{6,2},{7,3},{8,12},{9,13},{10,... | collective-permute-start | bytes 221192 | tf_op jit(solution)/shard_map/ppermute | solution.py:329
  91.4 5.0 %collective-permute-start.14 = (f32[9,16,128]{2,1,0:T(8,128)S(1)}, f32[9,16,128]{2,1,0:T(8,128)S(1)}, u32[]{:S(2)}, u32[]{:S(2)}) collective-permute-start(f32[9,16,128]{2,1,0:T(8,128)S(1)} %add_add_fusion.2), channel_id=1, source_target_pairs={{0,6},{1,7},{2,4},{3,5},{4,2},{5,3},{6,0},{7,1},{8,14},{9,15},{10,... | collective-permute-start | bytes 221192 | tf_op jit(solution)/shard_map/ppermute | solution.py:329
  93.1 4.2 %collective-permute-start.12 = (f32[9,16,128]{2,1,0:T(8,128)S(1)}, f32[9,16,128]{2,1,0:T(8,128)S(1)}, u32[]{:S(2)}, u32[]{:S(2)}) collective-permute-start(f32[9,16,128]{2,1,0:T(8,128)S(1)} %add_add_fusion.2), channel_id=1, source_target_pairs={{0,2},{1,3},{2,0},{3,1},{4,6},{5,7},{6,4},{7,5},{8,10},{9,11},{10,... | collective-permute-start | bytes 221192 | tf_op jit(solution)/shard_map/ppermute | solution.py:329
  97.4 5.8 %collective-permute-start.16 = (f32[9,16,128]{2,1,0:T(8,128)S(1)}, f32[9,16,128]{2,1,0:T(8,128)S(1)}, u32[]{:S(2)}, u32[]{:S(2)}) collective-permute-start(f32[9,16,128]{2,1,0:T(8,128)S(1)} %add_add_fusion.1), channel_id=1, source_target_pairs={{0,16},{1,17},{2,18},{3,19},{4,20},{5,21},{6,22},{7,23},{8,24},{9,... | collective-permute-start | bytes 221192 | tf_op jit(solution)/shard_map/ppermute | solution.py:329
  100.3 4.4 %collective-permute-start.17 = (f32[9,16,128]{2,1,0:T(8,128)S(1)}, f32[9,16,128]{2,1,0:T(8,128)S(1)}, u32[]{:S(2)}, u32[]{:S(2)}) collective-permute-start(f32[9,16,128]{2,1,0:T(8,128)S(1)} %add_add_fusion.1), channel_id=1, source_target_pairs={{0,24},{1,25},{2,26},{3,27},{4,28},{5,29},{6,30},{7,31},{8,16},{9,... | collective-permute-start | bytes 221192 | tf_op jit(solution)/shard_map/ppermute | solution.py:329
  100.3 4.4 %collective-permute-start.15 = (f32[9,16,128]{2,1,0:T(8,128)S(1)}, f32[9,16,128]{2,1,0:T(8,128)S(1)}, u32[]{:S(2)}, u32[]{:S(2)}) collective-permute-start(f32[9,16,128]{2,1,0:T(8,128)S(1)} %add_add_fusion.1), channel_id=1, source_target_pairs={{0,8},{1,9},{2,10},{3,11},{4,12},{5,13},{6,14},{7,15},{8,0},{9,1},... | collective-permute-start | bytes 221192 | tf_op jit(solution)/shard_map/ppermute | solution.py:329
  100.4 16.0 %collective-permute-start.22 = (f32[2,2,128,256]{3,2,1,0:T(8,128)S(1)}, f32[2,2,128,256]{3,2,1,0:T(8,128)S(1)}, u32[]{:S(2)}, u32[]{:S(2)}) collective-permute-start(f32[2,2,128,256]{3,2,1,0:T(8,128)S(1)} %add_dynamic-update-slice_fusion.2), channel_id=1, source_target_pairs={{0,32},{32,64},{64,96},{1,33},{33,65},{65,97},{2,34},{34,66},{66,9... | collective-permute-start | bytes 1572872 | tf_op jit(solution)/shard_map/ppermute | solution.py:283
  105.8 9.1 %collective-permute-start.19 = (f32[8,16,128]{2,1,0:T(8,128)S(1)}, f32[8,16,128]{2,1,0:T(8,128)S(1)}, u32[]{:S(2)}, u32[]{:S(2)}) collective-permute-start(f32[8,16,128]{2,1,0:T(8,128)S(1)} %get-tuple-element.119), channel_id=1, source_target_pairs={{0,32},{1,33},{2,34},{3,35},{4,36},{5,37},{6,38},{7,39},{8,40},{9,... | collective-permute-start | bytes 196616 | tf_op jit(solution)/shard_map/ppermute | solution.py:339
  106.7 9.6 %collective-permute-start.20 = (f32[8,16,128]{2,1,0:T(8,128)S(1)}, f32[8,16,128]{2,1,0:T(8,128)S(1)}, u32[]{:S(2)}, u32[]{:S(2)}) collective-permute-start(f32[8,16,128]{2,1,0:T(8,128)S(1)} %get-tuple-element.119), channel_id=1, source_target_pairs={{0,64},{1,65},{2,66},{3,67},{4,68},{5,69},{6,70},{7,71},{8,72},{9,... | collective-permute-start | bytes 196616 | tf_op jit(solution)/shard_map/ppermute | solution.py:339
  108.8 7.5 %collective-permute-start.21 = (f32[8,16,128]{2,1,0:T(8,128)S(1)}, f32[8,16,128]{2,1,0:T(8,128)S(1)}, u32[]{:S(2)}, u32[]{:S(2)}) collective-permute-start(f32[8,16,128]{2,1,0:T(8,128)S(1)} %get-tuple-element.119), channel_id=1, source_target_pairs={{0,96},{1,97},{2,98},{3,99},{4,100},{5,101},{6,102},{7,103},{8,104... | collective-permute-start | bytes 196616 | tf_op jit(solution)/shard_map/ppermute | solution.py:339
  116.4 6.3 %collective-permute-start.23 = (f32[8,64,128]{2,1,0:T(8,128)S(1)}, f32[8,64,128]{2,1,0:T(8,128)S(1)}, u32[]{:S(2)}, u32[]{:S(2)}) collective-permute-start(f32[8,64,128]{2,1,0:T(8,128)S(1)} %constant_dynamic-update-slice_fusion), channel_id=1, source_target_pairs={{0,1},{1,0},{2,3},{3,2},{4,5},{5,4},{6,7},{7,6},{8,9},{9,8},{10,11... | collective-permute-start | bytes 786440 | tf_op jit(solution)/shard_map/ppermute | solution.py:348
  (12 other events, 90.0 us)
